TPU v7x, 256 devices: a whole 4x4x8 slice. The times are simulated.
256 devices in a mesh: row: 16 (over x, z_lo), col: 16 (over y, z_hi, core).
Axes of the slice: x: 4, y: 4, z: 8 (z_hi: 2, z_lo: 4; z = z_hi * 4 + z_lo), core: 2. Of those that a mesh axis runs over, the one named last changes fastest.
Arguments:
- homolog_tensor: bfloat16 [512, 256, 256], P('row', 'col'), may hold values from -6 to 6
- pairwise_tensor: bfloat16 [256, 256, 128], P('row', 'col'), may hold values from -6 to 6
- genuine_amino_flags: int32 [256], replicated, may hold values 0 or 1
- polymer_identity: int32 [256], replicated, may hold values from 0 to 3, never falling along the last dimension, each value on 1 to 128 neighbouring positions
- asking_weights: bfloat16 [256, 256], replicated, may hold values from -0.375 to 0.375
- attend_sigmoid_weights: bfloat16 [256, 256], replicated, may hold values from -0.375 to 0.375
- lookup_content_weights: bfloat16 [256, 512], replicated, may hold values from -0.375 to 0.375
- attend_final_weights: bfloat16 [256, 256], replicated, may hold values from -0.375 to 0.375
- pairwise_logit_weights: bfloat16 [128, 8], replicated, may hold values from -20 to 20
- crosspolymer_offset: float32 [8], replicated, may hold values from -2 to 2
- outgoing_link_weights: bfloat16 [128, 256], replicated, may hold values from -0.5 to 0.5
- incoming_link_weights: bfloat16 [128, 256], replicated, may hold values from -0.5 to 0.5
- trimult_sigmoid_weights: bfloat16 [128, 128], replicated, may hold values from -0.5 to 0.5
- trimult_final_weights: bfloat16 [128, 128], replicated, may hold values from -0.5 to 0.5
Outputs:
- attended_homologs: bfloat16 [512, 256, 256], P('row', 'col')
- pair_output: bfloat16 [256, 256, 128], P('row', 'col')
Inputs may be any that keep to these rules, and one draw needn't show every extreme that they name: `polymer_identity`: chain ids never fall along the residues; each chain has 1 to 128 residues and one has exactly that many.
All inputs are finite; a program needn't handle non-finite values.
Results may differ from a plain program's by a relative error of at most 0.0035.
The roundings to bfloat16 on the way count: a program that leaves them out, or rounds other values in their place, can miss the bound.
Values may be sent and summed in bfloat16 or wider, within the bound.
No kernel may reach another device: no remote copies, remote signals or barrier semaphores. Data moves between devices by JAX's collectives and lax.ppermute only.
A program may use at most 64 MiB of HBM per device.

v0:
```python
import jax
import jax.numpy as jnp
from jax import lax
from jax.sharding import PartitionSpec as P


def from_root(array, axis, root):
    mine = lax.axis_index(axis) == root
    return lax.psum(jnp.where(mine, array, jnp.zeros_like(array)), axis)


def standardize_features(tensor):
    tensor = tensor.astype(jnp.float32)
    center = tensor - jnp.mean(tensor, axis=-1, keepdims=True)
    spread = jnp.mean(center * center, axis=-1, keepdims=True)
    return center * lax.rsqrt(spread + 1e-05)


def edges(pair_norm, weight, mask_rows, width):
    projected = jnp.dot(pair_norm, weight, preferred_element_type=jnp.float32)
    edge_vals = (
        mask_rows * jax.nn.sigmoid(projected[..., :width]) * projected[..., width:]
    ).astype(jnp.bfloat16)
    return jnp.transpose(edge_vals, (2, 0, 1))


def local(
    homolog_tensor,
    pairwise_tensor,
    genuine_amino_flags,
    polymer_identity,
    asking_weights,
    attend_sigmoid_weights,
    lookup_content_weights,
    attend_final_weights,
    pairwise_logit_weights,
    crosspolymer_offset,
    outgoing_link_weights,
    incoming_link_weights,
    trimult_sigmoid_weights,
    trimult_final_weights,
):
    row_count = lax.axis_size("row")
    col_count = lax.axis_size("col")
    row_index = lax.axis_index("row")
    col_index = lax.axis_index("col")
    homolog_entries, amino_positions, feature_depth = homolog_tensor.shape
    res_rows = pairwise_tensor.shape[0]
    pair_width = pairwise_tensor.shape[2]
    row_ratio = row_count // col_count
    head_count = pairwise_logit_weights.shape[1]
    inner_width = asking_weights.shape[1]
    per_head_width = inner_width // head_count
    standardized_homologs = standardize_features(homolog_tensor).astype(jnp.bfloat16)
    pair_norm = standardize_features(pairwise_tensor).astype(jnp.bfloat16)
    local_bias = jnp.einsum(
        "ijc,ch->hij", pair_norm, pairwise_logit_weights, preferred_element_type=jnp.float32
    ).astype(jnp.bfloat16)
    row_bias = lax.all_gather(local_bias, "col", axis=2, tiled=True)
    queries = (
        jnp.dot(standardized_homologs, asking_weights, preferred_element_type=jnp.float32)
        * per_head_width ** (-0.5)
    ).astype(jnp.bfloat16)
    queries = queries.reshape(homolog_entries, amino_positions, head_count, per_head_width)
    gate_activation = jax.nn.sigmoid(
        jnp.dot(standardized_homologs, attend_sigmoid_weights, preferred_element_type=jnp.float32)
    )
    all_bias = lax.all_gather(row_bias, "row", axis=1, tiled=True)
    bias_block = lax.dynamic_slice_in_dim(all_bias, col_index * amino_positions, amino_positions, 1)
    query_chain = lax.dynamic_slice_in_dim(
        polymer_identity, col_index * amino_positions, amino_positions, 0
    )
    cross_chain = (query_chain[:, None] != polymer_identity[None, :]).astype(jnp.float32)
    extra_bias = (
        bias_block.astype(jnp.float32) + crosspolymer_offset[:, None, None] * cross_chain[None]
    )
    keep_all = genuine_amino_flags > 0
    key_value = jnp.dot(
        lax.all_gather(standardized_homologs, "col", axis=1, tiled=True),
        lookup_content_weights,
        preferred_element_type=jnp.float32,
    ).astype(jnp.bfloat16)
    piece_len = key_value.shape[1]
    key_rows = key_value[..., :inner_width].reshape(
        homolog_entries, piece_len, head_count, per_head_width
    )
    value_rows = key_value[..., inner_width:].reshape(
        homolog_entries, piece_len, head_count, per_head_width
    )
    scores = jnp.einsum("sqhd,skhd->shqk", queries, key_rows, preferred_element_type=jnp.float32)
    scores = scores + extra_bias[None]
    scores = jnp.where(keep_all, scores, -1000000000.0)
    peak_old = jnp.full((homolog_entries, head_count, amino_positions), -jnp.inf, jnp.float32)
    total_old = jnp.zeros((homolog_entries, head_count, amino_positions), jnp.float32)
    accum_old = jnp.zeros(
        (homolog_entries, head_count, amino_positions, per_head_width), jnp.float32
    )
    peak_now = jnp.max(scores, axis=-1)
    factor = jnp.exp(peak_old - peak_now)
    exp_scores = jnp.exp(scores - peak_now[..., None])
    total_now = total_old * factor + jnp.sum(exp_scores, axis=-1)
    accum_now = accum_old * factor[..., None] + jnp.einsum(
        "shqk,skhd->shqd",
        exp_scores.astype(jnp.bfloat16),
        value_rows,
        preferred_element_type=jnp.float32,
    )
    peak_now, total_now, accum_now = (peak_now, total_now, accum_now)
    attended = accum_now / total_now[..., None]
    attended = jnp.transpose(attended, (0, 2, 1, 3)).reshape(
        homolog_entries, amino_positions, inner_width
    )
    gated_output = (gate_activation * attended).astype(jnp.bfloat16)
    attended_homologs = (
        homolog_tensor.astype(jnp.float32)
        + jnp.dot(gated_output, attend_final_weights, preferred_element_type=jnp.float32)
    ).astype(jnp.bfloat16)
    mask_rows = lax.dynamic_slice_in_dim(
        genuine_amino_flags, row_index * res_rows, res_rows, 0
    ).astype(jnp.float32)[:, None, None]
    left_tri = edges(pair_norm, outgoing_link_weights, mask_rows, pair_width)
    right_tri = edges(pair_norm, incoming_link_weights, mask_rows, pair_width)
    left_cols = lax.all_gather(left_tri, "row", axis=1, tiled=True)
    left_mine = from_root(left_cols, "col", row_index // row_ratio)
    product = jnp.einsum(
        "cki,ckj->cij",
        left_mine,
        lax.all_gather(right_tri, "row", axis=1, tiled=True),
        preferred_element_type=jnp.float32,
    )
    product_norm = standardize_features(jnp.transpose(product, (1, 2, 0))).astype(jnp.bfloat16)
    tri_gate = jax.nn.sigmoid(
        jnp.dot(pair_norm, trimult_sigmoid_weights, preferred_element_type=jnp.float32)
    )
    update = jnp.dot(product_norm, trimult_final_weights, preferred_element_type=jnp.float32)
    pair_output = (pairwise_tensor.astype(jnp.float32) + tri_gate * update).astype(jnp.bfloat16)
    return (attended_homologs, pair_output)


def solution(mesh):
    in_specs = (
        P("row", "col", None),
        P("row", "col", None),
        P(),
        P(),
        P(),
        P(),
        P(),
        P(),
        P(),
        P(),
        P(),
        P(),
        P(),
        P(),
    )
    out_specs = (P("row", "col", None), P("row", "col", None))
    return jax.shard_map(local, mesh=mesh, in_specs=in_specs, out_specs=out_specs, check_vma=False)
```

profile of v0, /device:TPU:1, one launch (start us, length us, event | category | flops | bytes accessed | tf_op | source)
XLA Modules:
  0.0 572.7 jit_solution(12482841881399807148)
XLA Ops:
  7.2 1.0 convert_reduce_fusion.1
  8.2 1.0 fusion.36
  9.3 1.2 fusion.53
  10.5 1.1 fusion.55
  11.6 0.8 dynamic-slice_convert_fusion
  12.4 0.8 fusion.60
  13.1 0.0 all-gather.7.cloned.1.call-start
  13.2 1.2 fusion.23
  14.4 0.1 copy.43
  14.5 40.5 %all_gather.16 = bf16[8,16,256]{1,0,2:T(8,128)(2,1)S(1)} all-gather(bf16[8,16,16]{1,0,2:T(8,128)(2,1)S(1)} %copy.43), channel_id=1, replica_groups=mesh['row'=16,'col'=16] {'col'}, dimensions={2}, use_global_device_ids=true | all-gather | bytes 69632 | tf_op jit(solution)/shard_map/all_gather | solution.py:59
  55.0 1.0 copy.44
  56.0 0.0 all-gather.11.cloned.1.call-start
  56.0 0.7 all-gather.11.cloned.1.call-update
  56.7 0.0 all-reduce.2.cloned.1.call-start
  56.8 36.2 %all-gather.9.cloned.1.call-done = bf16[128,256,16]{0,2,1:T(8,128)(2,1)} async-done(((bf16[128,16,16]{0,2,1:T(8,128)(2,1)}), bf16[128,256,16]{0,2,1:T(8,128)(2,1)}) %all-gather.9.cloned.1.call-update) | async-done | bytes 1048592 | tf_op jit(solution)/shard_map/all_gather | solution.py:123
  93.0 2.2 copy.48
  95.2 1.1 broadcast_select_fusion
  96.3 0.2 all-gather.5.cloned.1.call-start
  96.6 0.1 convert_reduce_fusion
  96.7 0.2 fusion.30
  97.0 0.9 fusion.31
  97.9 0.3 fusion.15
  98.3 0.4 reshape.94
  98.7 0.1 dynamic_slice.10
  98.8 0.1 compare_convert_fusion
  98.9 75.5 %all-gather.7.cloned.1.call-done = bf16[8,256,256]{2,0,1:T(8,128)(2,1)} async-done(((bf16[8,16,256]{2,0,1:T(8,128)(2,1)}), bf16[8,256,256]{2,0,1:T(8,128)(2,1)}) %all-gather.7.cloned.1.call-update) | async-done | bytes 1048592 | tf_op jit(solution)/shard_map/all_gather | solution.py:68
  174.4 0.9 multiply_add_fusion
  175.3 81.6 %all-gather.11.cloned.1.call-done = bf16[128,256,16]{0,2,1:T(8,128)(2,1)} async-done(((bf16[128,16,16]{0,2,1:T(8,128)(2,1)}), bf16[128,256,16]{0,2,1:T(8,128)(2,1)}) %all-gather.11.cloned.1.call-update) | async-done | bytes 1048592 | tf_op jit(solution)/shard_map/all_gather | solution.py:128
  257.0 7.6 %copy.49 = bf16[128,256,16]{2,1,0:T(8,128)(2,1)} copy(bf16[128,256,16]{0,2,1:T(8,128)(2,1)} %all-gather.11.cloned.1.call-done) | data formatting | bytes 2097152 | tf_op jit(solution)/shard_map/all_gather | solution.py:128
  264.5 183.6 %all-reduce.2.cloned.1.call-done = bf16[128,256,16]{1,2,0:T(8,128)(2,1)} async-done(((bf16[128,256,16]{1,2,0:T(8,128)(2,1)}), bf16[128,256,16]{1,2,0:T(8,128)(2,1)}) %all-reduce.2.cloned.1.call-update) | async-done | bytes 1048592 | tf_op jit(solution)/shard_map/psum | solution.py:9
  448.2 4.9 fusion.74
  453.1 0.4 copy.50
  453.5 0.1 bitcast_reduce_fusion
  453.6 0.2 multiply_reduce_fusion
  453.9 0.2 fusion.52
  454.1 0.9 fusion.22
  455.0 76.2 %all-gather.5.cloned.1.call-done = bf16[32,256,256]{2,1,0:T(8,128)(2,1)} async-done(((bf16[32,16,256]{2,1,0:T(8,128)(2,1)}), bf16[32,256,256]{2,1,0:T(8,128)(2,1)}) %all-gather.5.cloned.1.call-update) | async-done | bytes 4194320 | tf_op jit(solution)/shard_map/all_gather | solution.py:79
  531.2 4.5 convolution_convert_fusion
  535.8 3.6 fusion.73
  539.3 6.5 %copy.41 = bf16[32,256,256]{1,2,0:T(8,128)(2,1)} copy(bf16[32,256,256]{2,1,0:T(8,128)(2,1)} %get-tuple-element.3) | data formatting | bytes 8388608 | tf_op jit(solution)/shard_map/slice | solution.py:84
  545.8 3.2 fusion
  549.0 1.9 copy-done.1
  550.9 1.5 fusion.1
  552.5 6.5 %copy.46 = bf16[32,256,256]{1,2,0:T(8,128)(2,1)} copy(bf16[32,256,256]{2,1,0:T(8,128)(2,1)} %get-tuple-element.2) | data formatting | bytes 8388608 | tf_op jit(solution)/shard_map/slice | solution.py:87
  559.0 4.5 fusion.5
  563.5 0.9 copy.47
  564.4 0.6 reshape.97
  565.0 1.2 fusion.16
  (38 shorter events, 0.3 us)
Async XLA Ops:
  7.2 524.1 %copy-start = (bf16[256,512]{1,0:T(8,128)(2,1)S(1)}, bf16[256,512]{1,0:T(8,128)(2,1)}, u32[]{:S(2)}) copy-start(bf16[256,512]{1,0:T(8,128)(2,1)} %param.20) | copy-start | bytes 786436
  7.2 85.9 %all-gather.9.cloned.1.call-start = ((), (), s32[]{:S(2)}) async-start(), calls=%async_computation.2 | async-start | bytes 1114112 | tf_op jit(solution)/shard_map/all_gather | solution.py:123
  9.3 87.3 %copy-start.2 = (bf16[32,16,256]{2,1,0:T(8,128)(2,1)S(1)}, bf16[32,16,256]{2,1,0:T(8,128)(2,1)}, u32[]{:S(2)}) copy-start(bf16[32,16,256]{2,1,0:T(8,128)(2,1)} %param.14) | copy-start | bytes 786436
  13.1 84.8 %copy-start.7 = (bf16[256,256]{1,0:T(8,128)(2,1)S(1)}, bf16[256,256]{1,0:T(8,128)(2,1)}, u32[]{:S(2)}) copy-start(bf16[256,256]{1,0:T(8,128)(2,1)} %param.18) | copy-start | bytes 393220
  13.1 161.2 %all-gather.7.cloned.1.call-start = ((), (), s32[]{:S(2)}) async-start(), calls=%async_computation.1 | async-start | bytes 1114112 | tf_op jit(solution)/shard_map/all_gather | solution.py:68
  56.0 201.0 %all-gather.11.cloned.1.call-start = ((), (), s32[]{:S(2)}) async-start(), calls=%async_computation.4 | async-start | bytes 1114112 | tf_op jit(solution)/shard_map/all_gather | solution.py:128
  56.7 391.5 %all-reduce.2.cloned.1.call-start = ((), (), s32[]{:S(2)}) async-start(), calls=%async_computation.3 | async-start | bytes 2097152 | tf_op jit(solution)/shard_map/psum | solution.py:9
  56.8 42.0 %copy-start.5 = (s32[256]{0:T(256)S(1)}, s32[256]{0:T(256)}, u32[]{:S(2)}) copy-start(s32[256]{0:T(256)} %param.17) | copy-start | bytes 3076
  56.8 42.0 %copy-start.11 = (s32[256]{0:T(256)S(1)}, s32[256]{0:T(256)}, u32[]{:S(2)}) copy-start(s32[256]{0:T(256)} %param.16) | copy-start | bytes 3076
  56.8 117.6 %copy-start.6 = (f32[8]{0:T(128)S(1)}, f32[8]{0:T(128)}, u32[]{:S(2)}) copy-start(f32[8]{0:T(128)} %param.23) | copy-start | bytes 100
  96.3 434.9 %all-gather.5.cloned.1.call-start = ((), (), s32[]{:S(2)}) async-start(), calls=%async_computation | async-start | bytes 4456448 | tf_op jit(solution)/shard_map/all_gather | solution.py:79
  264.5 189.3 %copy-start.4 = (bf16[128,128]{1,0:T(8,128)(2,1)S(1)}, bf16[128,128]{1,0:T(8,128)(2,1)}, u32[]{:S(2)}) copy-start(bf16[128,128]{1,0:T(8,128)(2,1)} %param.27) | copy-start | bytes 98308
  264.5 189.6 %copy-start.3 = (bf16[16,16,128]{2,1,0:T(8,128)(2,1)S(1)}, bf16[16,16,128]{2,1,0:T(8,128)(2,1)}, u32[]{:S(2)}) copy-start(bf16[16,16,128]{2,1,0:T(8,128)(2,1)} %param.15) | copy-start | bytes 196612
  264.5 189.6 %copy-start.10 = (bf16[128,128]{1,0:T(8,128)(2,1)S(1)}, bf16[128,128]{1,0:T(8,128)(2,1)}, u32[]{:S(2)}) copy-start(bf16[128,128]{1,0:T(8,128)(2,1)} %param.26) | copy-start | bytes 98308
  549.0 1.9 copy-start.1
  563.5 1.5 copy-start.8
  563.5 1.5 copy-start.9
Sparse Core Ops, SparseCore 0:
  13.3 79.7 all-gather.8
  95.4 78.9 all-gather.6
  176.2 80.7 all-gather.10
  259.5 188.6 all-reduce.1
  451.5 79.7 all-gather.4
where the time goes:
time: 574 us; the launch traced here: 573 us
  waiting for transfers between devices  454 us (79%)
  blocking collectives  40.5 us (7%)
  local copies, waits for them, and re-layouts  31.8 us (6%)
  matrix products  23.2 us (4%)
  between operations  14.1 us (2%)
  other arithmetic  8.8 us (2%)
    psum x1, waiting for transfers between devices, from_root(): return lax.psum(jnp.where(mine, array, jnp.zeros_like(array)), axis)  184 us
    all_gather x1, waiting for transfers between devices, local(): lax.all_gather(right_tri, 'row', axis=1, tiled=True)  81.6 us
    all_gather x1, waiting for transfers between devices, local(): lax.all_gather(standardized_homologs, 'col', axis=1, tiled=True)  76.2 us
    all_gather x1, waiting for transfers between devices, local(): all_bias = lax.all_gather(row_bias, 'row', axis=1, tiled=True)  75.5 us
    all_gather x1, blocking collectives, local(): row_bias = lax.all_gather(local_bias, 'col', axis=2, tiled=True)  40.5 us
    all_gather x1, waiting for transfers between devices, local(): left_cols = lax.all_gather(left_tri, 'row', axis=1, tiled=True)  36.2 us
  transfers between devices with their start and end apart: 5, of which 5 were waited for; matrix products, arithmetic and copies ran while one was open for 4% of the time, Pallas kernels for 0%

commit v1 on v0

v1 whole, which is shorter than its diff:
```python
import jax
import jax.numpy as jnp
from jax import lax
from jax.sharding import PartitionSpec as P

AXES = ("row", "col")
F32 = jnp.float32
BF16 = jnp.bfloat16


def standardize(tensor):
    tensor = tensor.astype(F32)
    center = tensor - jnp.mean(tensor, axis=-1, keepdims=True)
    spread = jnp.mean(center * center, axis=-1, keepdims=True)
    return center * lax.rsqrt(spread + 1e-05)


def dot(a, b):
    return jnp.dot(a, b, preferred_element_type=F32)


def pre(homolog, pair, row_flags, w_q, w_kv, w_bias, w_out, w_in):
    seqs, res, depth = homolog.shape
    heads = w_bias.shape[1]
    width = w_q.shape[1]
    dh = width // heads
    cz = pair.shape[-1]
    msa_norm = standardize(homolog).astype(BF16)
    pair_norm = standardize(pair).astype(BF16)
    queries = (dot(msa_norm, w_q) * dh**-0.5).astype(BF16)
    key_value = dot(msa_norm, w_kv).astype(BF16)
    qkv = jnp.concatenate(
        [a.reshape(seqs, res, heads, dh) for a in (queries, key_value[..., :width], key_value[..., width:])],
        axis=-1,
    )
    qkv = jnp.transpose(qkv, (2, 0, 1, 3)).reshape(heads * seqs, res, 3 * dh)
    bias = jnp.transpose(dot(pair_norm, w_bias).astype(BF16), (2, 0, 1))
    bias = jnp.broadcast_to(bias[:, None], (heads, seqs, res, res)).reshape(heads * seqs, res, res)

    def edges(weight):
        projected = dot(pair_norm, weight)
        edge = row_flags.astype(F32)[:, None, None] * jax.nn.sigmoid(projected[..., :cz]) * projected[..., cz:]
        edge = edge.astype(BF16).reshape(2, res // 2, res, cz)
        return jnp.transpose(edge, (0, 3, 1, 2)).reshape(2 * cz, res // 2, res)

    tri = jnp.concatenate([edges(w_out), edges(w_in)], axis=1)
    return jnp.concatenate([qkv, bias, tri], axis=-1), msa_norm, pair_norm


def mid(received, flags, chain, offset):
    n = 16
    x = received.reshape(n, n * n, 128)
    q, k, v = x[..., :32], x[..., 32:64], x[..., 64:96]
    tiles = received.reshape(n, n, 16, 128)
    bias = jnp.transpose(tiles[..., 96:112], (0, 2, 1, 3)).reshape(256, 256)
    tri = tiles[..., 112:]
    left = jnp.transpose(tri[:, :, :8], (0, 2, 1, 3)).reshape(128, 256)
    right = jnp.transpose(tri[:, :, 8:], (0, 2, 1, 3)).reshape(128, 256)
    cross = (chain[:, None] != chain[None, :]).astype(F32)
    extra = bias.astype(F32) + offset * cross
    scores = jnp.einsum("sid,sjd->sij", q, k, preferred_element_type=F32) + extra
    scores = jnp.where(flags > 0, scores, -1000000000.0)
    exp_scores = jnp.exp(scores - jnp.max(scores, axis=-1, keepdims=True))
    total = jnp.sum(exp_scores, axis=-1)
    attended = jnp.einsum("sij,sjd->sid", exp_scores.astype(BF16), v, preferred_element_type=F32)
    attended = (attended / total[..., None]).astype(BF16)
    product = lax.dot_general(left, right, (((0,), (0,)), ((), ())), preferred_element_type=F32)
    high = product.astype(BF16)
    rest = (product - high.astype(F32)).astype(BF16)

    def tiled(a):
        return jnp.transpose(a.reshape(n, 16, n, 16), (0, 2, 1, 3)).reshape(256, 16, 16)

    chunk = jnp.concatenate([attended.reshape(256, 16, 32), tiled(high), tiled(rest)], axis=-1)
    return jnp.concatenate([chunk[:, :8], chunk[:, 8:]], axis=-1)


def post(received, homolog, pair, msa_norm, pair_norm, w_gate, w_final, w_tri_gate, w_tri_final):
    seqs, res, depth = homolog.shape
    chunk = jnp.concatenate([received[..., :64], received[..., 64:]], axis=1)
    attended = chunk[..., :32].reshape(8, seqs, res, 32)
    attended = jnp.transpose(attended, (1, 2, 0, 3)).reshape(seqs, res, 256)
    gated = (jax.nn.sigmoid(dot(msa_norm, w_gate)) * attended.astype(F32)).astype(BF16)
    out = (homolog.astype(F32) + dot(gated, w_final)).astype(BF16)
    product = chunk[..., 32:48].astype(F32) + chunk[..., 48:64].astype(F32)
    product = jnp.transpose(product[:128] + product[128:], (1, 2, 0))
    product_norm = standardize(product).astype(BF16)
    update = jax.nn.sigmoid(dot(pair_norm, w_tri_gate)) * dot(product_norm, w_tri_final)
    return out, (pair.astype(F32) + update).astype(BF16)


def exchange(chunks):
    return lax.all_to_all(chunks, AXES, split_axis=0, concat_axis=0, tiled=True)


def local(
    homolog_tensor,
    pairwise_tensor,
    genuine_amino_flags,
    polymer_identity,
    asking_weights,
    attend_sigmoid_weights,
    lookup_content_weights,
    attend_final_weights,
    pairwise_logit_weights,
    crosspolymer_offset,
    outgoing_link_weights,
    incoming_link_weights,
    trimult_sigmoid_weights,
    trimult_final_weights,
):
    row = lax.axis_index("row")
    row_flags = lax.dynamic_slice_in_dim(genuine_amino_flags, row * 16, 16, 0)
    send, msa_norm, pair_norm = pre(
        homolog_tensor,
        pairwise_tensor,
        row_flags,
        asking_weights,
        lookup_content_weights,
        pairwise_logit_weights,
        outgoing_link_weights,
        incoming_link_weights,
    )
    back = mid(exchange(send), genuine_amino_flags, polymer_identity, crosspolymer_offset[row // 2])
    return post(
        exchange(back),
        homolog_tensor,
        pairwise_tensor,
        msa_norm,
        pair_norm,
        attend_sigmoid_weights,
        attend_final_weights,
        trimult_sigmoid_weights,
        trimult_final_weights,
    )


def solution(mesh):
    block = P("row", "col", None)
    in_specs = (block, block) + (P(),) * 12
    return jax.shard_map(local, mesh=mesh, in_specs=in_specs, out_specs=(block, block), check_vma=False)
```

time: 574 us -> 125 us (0.22)
  waiting for transfers between devices: 454 us -> 32 us
  starting transfers between devices: 0.38 us -> 15.7 us
  blocking collectives: 40.5 us -> 26.2 us
  between operations: 14.1 us -> 1.18 us
  matrix products: 23.2 us -> 13 us
  local copies, waits for them, and re-layouts: 31.8 us -> 22.6 us
    all_gather x4 -> x0, waiting for transfers between devices: 270 us -> none  [the longest x1 81.6 us: local(): lax.all_gather(right_tri, 'row', axis=1, tiled=True)]
    psum x1 -> x0, waiting for transfers between devices: 184 us -> none  [from_root(): return lax.psum(jnp.where(mine, array, jnp.zeros_like(array)), axis)]
    all_gather x1 -> x0, blocking collectives: 40.5 us -> none  [local(): row_bias = lax.all_gather(local_bias, 'col', axis=2, tiled=True)]
    all_to_all x0 -> x1, waiting for transfers between devices: none -> 32 us  [exchange(): return lax.all_to_all(chunks, AXES, split_axis=0, concat_axis=0, tiled=True)]
    all_to_all x0 -> x1, blocking collectives: none -> 26.2 us  [exchange(): return lax.all_to_all(chunks, AXES, split_axis=0, concat_axis=0, tiled=True)]
    all_to_all x0 -> x1, starting transfers between devices: none -> 15.7 us  [exchange(): return lax.all_to_all(chunks, AXES, split_axis=0, concat_axis=0, tiled=True)]
    slice x3, local copies, waits for them, and re-layouts: 16.5 us -> 1.02 us  [the longest x1 0.74 us: pre(): key_value[..., :width]]
    all_gather x3 -> x0, local copies, waits for them, and re-layouts: 10.7 us -> none  [the longest x1 7.56 us: local(): lax.all_gather(right_tri, 'row', axis=1, tiled=True)]
  transfers between devices with their start and end apart: 5 -> 1, of which waited for: 5 -> 1; matrix products, arithmetic and copies ran while one was open for 4% -> 0% of each run, Pallas kernels for 0% -> 0%
where the time goes in v1:
time: 125 us
  waiting for transfers between devices  32 us (26%)
  blocking collectives  26.2 us (21%)
  local copies, waits for them, and re-layouts  22.6 us (18%)
  starting transfers between devices  15.7 us (13%)
  other arithmetic  14 us (11%)
  matrix products  13 us (10%)
    all_to_all x1, waiting for transfers between devices, exchange(): return lax.all_to_all(chunks, AXES, split_axis=0, concat_axis=0, tiled=True)  32 us
    all_to_all x1, blocking collectives, exchange(): return lax.all_to_all(chunks, AXES, split_axis=0, concat_axis=0, tiled=True)  26.2 us
    all_to_all x1, starting transfers between devices, exchange(): return lax.all_to_all(chunks, AXES, split_axis=0, concat_axis=0, tiled=True)  15.7 us
    dot_general x8, matrix products, dot(): return jnp.dot(a, b, preferred_element_type=F32)  9.74 us
    convert_element_type x3, local copies, waits for them, and re-layouts, post(): attended.astype(F32)  5.36 us
    reshape x6, local copies, waits for them, and re-layouts, pre(): a.reshape(seqs, res, heads, dh)  5.24 us
  transfers between devices with their start and end apart: 1, of which 1 were waited for; matrix products, arithmetic and copies ran while one was open for 0% of the time, Pallas kernels for 0%

profile of v1, /device:TPU:1, one launch (start us, length us, event | category | flops | bytes accessed | tf_op | source)
XLA Modules:
  0.0 124.6 jit_solution(7467932835509489327)
XLA Ops:
  0.7 1.0 convert_reduce_fusion.1
  1.7 1.0 fusion.59
  2.7 1.1 fusion.78
  3.9 1.1 fusion.80
  5.0 0.8 dynamic-slice_convert_fusion
  6.1 0.9 copy.107
  7.1 1.1 convert_reduce_fusion
  8.2 1.2 fusion.39
  9.4 0.3 convolution_convert_fusion
  9.8 0.7 fusion.97
  10.5 0.4 reshape.142
  11.1 1.7 %reshape.143 = bf16[32,16,8,32]{3,2,1,0:T(8,128)(2,1)S(1)} reshape(bf16[32,16,256]{2,1,0:T(8,128)(2,1)} %get-tuple-element.11) | data formatting | bytes 524288 | tf_op jit(solution)/shard_map/reshape | solution.py:33
  12.9 1.2 copy.103
  14.0 2.0 %fusion.14 = bf16[32,16,256]{2,1,0:T(8,128)(2,1)} fusion(bf16[32,16,256]{2,1,0:T(8,128)(2,1)} %param.14, f32[32,16]{1,0:T(8,128)S(1)} %add_rsqrt_fusion, f32[32,16]{1,0:T(8,128)S(1)} %broadcast_multiply_fusion, bf16[256,256]{1,0:T(8,128)(2,1)} %param.18), kind=kOutput, calls=%fused_computation.20 | convolution fusion | flops 67895296 | bytes 659456 | tf_op jit(solution)/shard_map/dot_general | solution.py:19
  16.0 1.7 %reshape.141 = bf16[32,16,8,32]{3,2,1,0:T(8,128)(2,1)S(1)} reshape(bf16[32,16,256]{2,1,0:T(8,128)(2,1)} %fusion.14) | data formatting | bytes 524288 | tf_op jit(solution)/shard_map/reshape | solution.py:33
  17.9 0.3 fusion.22
  18.2 2.2 %pad_maximum_fusion = bf16[32,16,8,96]{3,1,0,2:T(8,128)(2,1)S(1)} fusion(bf16[32,16,8,32]{3,1,0,2:T(8,128)(2,1)} %copy.103, bf16[32,16,8,32]{3,1,0,2:T(8,128)(2,1)S(1)} %copy.102, bf16[32,16,8,32]{3,1,0,2:T(8,128)(2,1)S(1)} %copy.101), kind=kLoop, calls=%fused_computation.35 | loop fusion | flops 2359296 | bytes 1572864 | tf_op jit(solution)/shard_map/concatenate | solution.py:32
  20.6 2.0 %pad_maximum_fusion.1 = bf16[256,16,128]{2,1,0:T(8,128)(2,1)} fusion(bf16[256,16,16]{2,1,0:T(8,128)(2,1)S(1)} %copy.107, bf16[256,16,16]{2,1,0:T(8,128)(2,1)S(1)} %bitcast.91, bf16[256,16,96]{2,1,0:T(8,128)(2,1)S(1)} %bitcast.93), kind=kLoop, calls=%fused_computation.36 | loop fusion | flops 3145728 | bytes 2097152 | tf_op jit(solution)/shard_map/concatenate | solution.py:47
  22.5 15.7 %all-to-all-start = ((bf16[256,16,128]{2,1,0:T(8,128)(2,1)}), bf16[256,16,128]{2,1,0:T(8,128)(2,1)S(1)}, u32[]{:S(2)}, u32[]{:S(2)}) async-start(bf16[256,16,128]{2,1,0:T(8,128)(2,1)} %pad_maximum_fusion.1), calls=%async_computation | async-start | bytes 2097152 | tf_op jit(solution)/shard_map/all_to_all | solution.py:93
  38.2 0.6 dynamic_slice.7
  38.8 32.0 %all-to-all-done = bf16[256,16,128]{2,1,0:T(8,128)(2,1)S(1)} async-done(((bf16[256,16,128]{2,1,0:T(8,128)(2,1)}), bf16[256,16,128]{2,1,0:T(8,128)(2,1)S(1)}, u32[]{:S(2)}, u32[]{:S(2)}) %all-to-all-start) | async-done | bytes 1048608 | tf_op jit(solution)/shard_map/all_to_all | solution.py:93
  70.8 0.3 convert_bitcast_fusion
  71.2 1.4 %slice_bitcast_fusion = (bf16[16,8,16,16]{3,1,2,0:T(8,128)(2,1)}, bf16[16,8,16,16]{3,1,2,0:T(8,128)(2,1)}) fusion(bf16[16,16,16,128]{3,2,1,0:T(8,128)(2,1)S(1)} %bitcast.83), kind=kLoop, calls=%fused_computation.50 | loop fusion | bytes 262144 | tf_op jit(solution)/shard_map/transpose | solution.py:58
  72.6 0.7 copy.110
  73.2 1.5 %reshape.159 = f32[256,256]{1,0:T(8,128)} reshape(f32[16,16,16,16]{3,2,1,0:T(8,128)S(1)} %copy.110) | data formatting | bytes 524288 | tf_op jit(solution)/shard_map/convert_element_type | solution.py:60
  74.8 1.7 %select_add_fusion = f32[256,256]{1,0:T(8,128)S(1)} fusion(f32[256,256]{1,0:T(8,128)} %reshape.159, f32[]{:T(128)} %bitcast.17, s32[256]{0:T(256)S(1)} %copy-done.6), kind=kLoop, calls=%fused_computation.58 | loop fusion | flops 196608 | bytes 525316 | tf_op jit(solution)/shard_map/add | solution.py:60
  76.6 1.0 fusion
  77.6 0.9 fusion.1
  78.6 1.4 %fusion.32 = bf16[16,256,32]{1,2,0:T(8,128)(2,1)S(1)} fusion(f32[16,256,256]{1,2,0:T(8,128)S(1)} %get-tuple-element.15, f32[16,256]{1,0:T(8,128)S(1)} %get-tuple-element.14, f32[256,256]{0,1:T(8,128)S(1)} %copy.111, pred[256]{0:T(512)(128)(4,1)S(1)} %broadcast_compare_fusion, bf16[16,256,128]{2,1,0:T(8,128)(2,1)S(1)} %bitcast.85, f32[16,256]{1,0:T(8,128)S(1)} %fusion.1), kind=kOutput, calls=%fused_computation.39 | convolution fusion | flops 71565312 | bytes 5800192 | tf_op jit(solution)/shard_map/sij,sjd->sid/dot_general | solution.py:65
  80.0 0.5 copy.114
  80.6 0.5 reshape.153
  81.2 0.5 reshape.154
  81.7 0.9 subtract_convert_fusion
  82.5 0.7 reshape.155
  83.2 0.3 copy.117
  83.5 1.8 %reshape.157 = bf16[16,16,16,16]{3,2,1,0:T(8,128)(2,1)S(1)} reshape(bf16[256,256]{1,0:T(8,128)(2,1)} %get-tuple-element.2) | data formatting | bytes 262144 | tf_op jit(solution)/shard_map/reshape | solution.py:72
  85.3 0.3 copy.118
  85.6 1.0 pad_maximum_fusion.2
  86.6 0.3 pad_maximum_fusion.3
  86.9 26.2 %all_to_all.10 = bf16[256,8,128]{2,1,0:T(8,128)(2,1)S(1)} all-to-all(bf16[256,8,128]{2,1,0:T(8,128)(2,1)S(1)} %pad_maximum_fusion.3), channel_id=1, replica_groups=mesh['row'=16,'col'=16] {'row','col'}, dimensions={0} | all-to-all | bytes 1048576 | tf_op jit(solution)/shard_map/all_to_all | solution.py:93
  113.3 0.3 copy.126
  113.6 0.3 copy.127
  114.4 0.5 reshape.161
  114.9 2.8 %copy.121 = f32[32,16,8,32]{3,2,1,0:T(8,128)} copy(f32[32,16,8,32]{0,2,3,1:T(8,128)S(1)} %bitcast.86) | data formatting | bytes 1048576 | tf_op jit(solution)/shard_map/convert_element_type | solution.py:83
  117.6 2.1 %reshape.160 = f32[32,16,256]{2,1,0:T(8,128)S(1)} reshape(f32[32,16,8,32]{3,2,1,0:T(8,128)} %copy.121) | data formatting | bytes 1048576 | tf_op jit(solution)/shard_map/convert_element_type | solution.py:83
  119.8 1.0 fusion.77
  120.8 1.7 %fusion.21 = bf16[16,16,128]{2,1,0:T(8,128)(2,1)} fusion(f32[16,16,128]{2,1,0:T(8,128)S(1)} %fusion.77, bf16[16,16,128]{2,1,0:T(8,128)(2,1)S(1)} %copy-done.5, bf16[128,128]{1,0:T(8,128)(2,1)} %param.26, f32[16,16]{1,0:T(8,128)S(1)} %add_rsqrt_fusion.2, f32[16,16]{1,0:T(8,128)S(1)} %broadcast_multiply_fusion.2), kind=kOutput, calls=%fused_computation.28 | convolution fusion | flops 8749056 | bytes 296960 | tf_op jit(solution)/shard_map/dot_general | solution.py:19
  122.5 2.1 %fusion.15 = bf16[32,16,256]{2,1,0:T(8,128)(2,1)} fusion(f32[32,16,256]{2,1,0:T(8,128)S(1)} %reshape.160, bf16[32,16,256]{2,1,0:T(8,128)(2,1)S(1)} %copy-done.2, f32[32,16]{1,0:T(8,128)S(1)} %add_rsqrt_fusion, f32[32,16]{1,0:T(8,128)S(1)} %broadcast_multiply_fusion, bf16[256,256]{1,0:T(8,128)(2,1)} %param.21, bf16[256,256]{1,0:T(8,128)(2,1)} %param.19), kind=kOutput, calls=%fused_computation.21 | convolution fusion | flops 135790592 | bytes 1314816 | tf_op jit(solution)/shard_map/dot_general | solution.py:19
  (46 shorter events, 1.9 us)
Async XLA Ops:
  0.6 8.8 %copy-start = (bf16[256,512]{1,0:T(8,128)(2,1)S(1)}, bf16[256,512]{1,0:T(8,128)(2,1)}, u32[]{:S(2)}) copy-start(bf16[256,512]{1,0:T(8,128)(2,1)} %param.20) | copy-start | bytes 786436
  0.6 8.8 %copy-start.1 = (bf16[32,16,256]{2,1,0:T(8,128)(2,1)S(1)}, bf16[32,16,256]{2,1,0:T(8,128)(2,1)}, u32[]{:S(2)}) copy-start(bf16[32,16,256]{2,1,0:T(8,128)(2,1)} %param.14) | copy-start | bytes 786436
  11.1 6.7 %copy-start.5 = (bf16[16,16,128]{2,1,0:T(8,128)(2,1)S(1)}, bf16[16,16,128]{2,1,0:T(8,128)(2,1)}, u32[]{:S(2)}) copy-start(bf16[16,16,128]{2,1,0:T(8,128)(2,1)} %param.15) | copy-start | bytes 196612
  11.1 6.7 %copy-start.7 = (bf16[128,8]{0,1:T(8,128)(2,1)S(1)}, bf16[128,8]{0,1:T(8,128)(2,1)}, u32[]{:S(2)}) copy-start(bf16[128,8]{0,1:T(8,128)(2,1)} %param.22) | copy-start | bytes 6148
  20.4 17.8 %copy-start.9 = (f32[8]{0:T(128)S(1)}, f32[8]{0:T(128)}, u32[]{:S(2)}) copy-start(f32[8]{0:T(128)} %param.23) | copy-start | bytes 100
  20.4 18.4 %copy-start.8 = (s32[256]{0:T(256)S(1)}, s32[256]{0:T(256)}, u32[]{:S(2)}) copy-start(s32[256]{0:T(256)} %param.16) | copy-start | bytes 3076
  22.5 48.3 %all-to-all-start = ((bf16[256,16,128]{2,1,0:T(8,128)(2,1)}), bf16[256,16,128]{2,1,0:T(8,128)(2,1)S(1)}, u32[]{:S(2)}, u32[]{:S(2)}) async-start(bf16[256,16,128]{2,1,0:T(8,128)(2,1)} %pad_maximum_fusion.1), calls=%async_computation | async-start | bytes 2097152 | tf_op jit(solution)/shard_map/all_to_all | solution.py:93
  71.2 3.6 %copy-start.6 = (s32[256]{0:T(256)S(1)}, s32[256]{0:T(256)}, u32[]{:S(2)}) copy-start(s32[256]{0:T(256)} %param.17) | copy-start | bytes 3076
  78.6 1.9 %copy-start.4 = (bf16[16,8,16,16]{3,1,2,0:T(8,128)(2,1)S(1)}, bf16[16,8,16,16]{3,1,2,0:T(8,128)(2,1)}, u32[]{:S(2)}) copy-start(bf16[16,8,16,16]{3,1,2,0:T(8,128)(2,1)} %get-tuple-element.7) | copy-start | bytes 196612
  78.6 2.5 %copy-start.3 = (bf16[16,8,16,16]{3,1,2,0:T(8,128)(2,1)S(1)}, bf16[16,8,16,16]{3,1,2,0:T(8,128)(2,1)}, u32[]{:S(2)}) copy-start(bf16[16,8,16,16]{3,1,2,0:T(8,128)(2,1)} %get-tuple-element.6) | copy-start | bytes 196612
  114.9 7.6 %copy-start.2 = (bf16[32,16,256]{2,1,0:T(8,128)(2,1)S(1)}, bf16[32,16,256]{2,1,0:T(8,128)(2,1)}, u32[]{:S(2)}) copy-start(bf16[32,16,256]{2,1,0:T(8,128)(2,1)} %param.14) | copy-start | bytes 786436

commit v2 on v1

v2 whole, which is shorter than its diff:
```python
import jax
import jax.numpy as jnp
from jax import lax
from jax.experimental import pallas as pl
from jax.experimental.pallas import tpu as pltpu
from jax.sharding import PartitionSpec as P

AXES = ("row", "col")
F32 = jnp.float32
BF16 = jnp.bfloat16
N = 16
HEADS = 8
DH = 32
LANES = 128
VMEM = pl.BlockSpec(memory_space=pltpu.VMEM)
SMEM = pl.BlockSpec(memory_space=pltpu.SMEM)
NT = (((1,), (1,)), ((), ()))
TN = (((0,), (0,)), ((), ()))


def standardize(tensor):
    tensor = tensor.astype(F32)
    center = tensor - jnp.mean(tensor, axis=-1, keepdims=True)
    spread = jnp.mean(center * center, axis=-1, keepdims=True)
    return center * lax.rsqrt(spread + 1e-05)


def dot(a, b, dims=(((1,), (0,)), ((), ()))):
    return lax.dot_general(a, b, dims, preferred_element_type=F32)


def lanes(shape):
    return lax.broadcasted_iota(jnp.int32, shape, len(shape) - 1)


def turn(x, by):
    by = by % LANES
    return x if by == 0 else pltpu.roll(x, by, x.ndim - 1)


def pre_kernel(flags_ref, x_ref, pair_ref, wq_ref, wkv_ref, wb_ref, wo_ref, wi_ref, send_ref, msa_ref, pn_ref, tri_ref, bias_ref):
    row = lax.axis_index("row")
    pair_norm = standardize(pair_ref[...].reshape(N * N, LANES)).astype(BF16)
    pn_ref[...] = pair_norm
    for w_ref, first in ((wo_ref, 0), (wi_ref, 8)):
        projected = dot(pair_norm, w_ref[...])
        edge = (jax.nn.sigmoid(projected[:, :LANES]) * projected[:, LANES:]).T
        for k in range(N):
            half, k8 = k // 8, k % 8
            flag = flags_ref[row * N + k].astype(F32)
            part = turn(edge[:, half * LANES : (half + 1) * LANES], 112 - k8 * 16) * flag
            tri_ref[pl.ds(half * 2048 + first + k8, LANES, stride=16), :] = part
    wb = jnp.concatenate([wb_ref[...].astype(F32), jnp.zeros((LANES, LANES - HEADS), F32)], axis=1).T
    bias = dot(wb[:HEADS].astype(BF16), pair_norm, NT)
    for i in range(N):
        half, i8 = i // 8, i % 8
        bias_ref[pl.ds(i, HEADS, stride=16), :] = turn(bias[:, half * LANES : (half + 1) * LANES], 96 - i8 * 16)

    msa_norm = standardize(x_ref[...].reshape(512, 256)).astype(BF16)
    msa_ref[...] = msa_norm
    lane = lanes((512, LANES))
    for h in range(HEADS):
        cut = slice(h * DH, (h + 1) * DH)
        cut_v = slice(256 + h * DH, 256 + (h + 1) * DH)
        weight = jnp.concatenate([wq_ref[:, cut], wkv_ref[:, cut], wkv_ref[:, cut_v], wq_ref[:, cut]], axis=1)
        y = dot(msa_norm, weight)
        y = jnp.where(lane < DH, y * DH**-0.5, y)
        bias_h = bias_ref[h * 16 : (h + 1) * 16, :]
        bias_h = jnp.broadcast_to(bias_h[None], (32, 16, LANES)).reshape(512, LANES)
        tri = tri_ref[h * 512 : (h + 1) * 512, :]
        out = jnp.where(lane < 96, y, jnp.where(lane < 112, bias_h, tri))
        send_ref[h * 512 : (h + 1) * 512, :] = out.astype(BF16)


def pre(homolog, pair, flags, w_q, w_kv, w_bias, w_out, w_in):
    return pl.pallas_call(
        pre_kernel,
        out_shape=(
            jax.ShapeDtypeStruct((4096, LANES), BF16),
            jax.ShapeDtypeStruct((512, 256), BF16),
            jax.ShapeDtypeStruct((256, LANES), BF16),
        ),
        in_specs=[SMEM] + [VMEM] * 7,
        out_specs=(VMEM, VMEM, VMEM),
        scratch_shapes=[pltpu.VMEM((4096, LANES), F32), pltpu.VMEM((LANES, LANES), F32)],
        compiler_params=pltpu.CompilerParams(vmem_limit_bytes=32 * 2**20),
        name="pre",
    )(flags, homolog, pair, w_q, w_kv, w_bias, w_out, w_in)


def mid_kernel(offset_ref, flags_ref, chain_ref, x_ref, out_ref, ps_ref):
    offset = offset_ref[lax.axis_index("row") // 2]
    wide = (256, LANES)
    slot = lanes(wide) // 16
    bias_cols, tri_cols = [], []
    for half in range(2):
        kept = [None, None]
        for c8 in range(8):
            starts = [(r * N + half * 8 + c8) * 16 for r in range(N)]
            part = jnp.concatenate([x_ref[s : s + 16, :] for s in starts], axis=0).astype(F32)
            part = turn(part, c8 * 16 - 96)
            old = kept[c8 % 2]
            pair_slots = (slot == c8) | (slot == (c8 + 1) % 8)
            kept[c8 % 2] = part if old is None else jnp.where(pair_slots, part, old)
        even = slot % 2 == 0
        bias_cols.append(jnp.where(even, kept[0], kept[1]))
        tri_cols.append(turn(jnp.where(even, kept[1], kept[0]), -16))
    bias = jnp.concatenate(bias_cols, axis=1)
    tri = jnp.concatenate(tri_cols, axis=1).reshape(N, 2, 8, 256)
    left = tri[:, 0].reshape(LANES, 256).T.astype(BF16)
    right = tri[:, 1].reshape(LANES, 256).astype(BF16)
    product = dot(left, right)
    high = product.astype(BF16).astype(F32)
    rest = product - high
    slot8 = lanes((LANES, LANES)) // 16

    for half in range(2):
        cols = slice(half * LANES, (half + 1) * LANES)
        high4 = high[:, cols].reshape(N, 2, 8, LANES)
        rest4 = rest[:, cols].reshape(N, 2, 8, LANES)
        upper = [(high4[:, u].reshape(LANES, LANES), turn(rest4[:, u].reshape(LANES, LANES), 16)) for u in range(2)]
        for parity in range(2):
            ours = slot8 % 2 == parity
            part_a = jnp.where(ours, *upper[0])
            part_b = turn(jnp.where(ours, *upper[1]), 64)
            near = (slot8 >= parity) & (slot8 < parity + 4)
            for merged, firsts in (
                (jnp.where(near, part_a, part_b), (parity, parity + 2)),
                (jnp.where(near, part_b, part_a), (parity + 4, parity + 6)),
            ):
                for c8 in firsts:
                    ps_ref[half * 8 + c8] = turn(merged, 32 - c8 * 16).reshape(N, 8, LANES)

    chain = jnp.broadcast_to(chain_ref[...].astype(F32), (LANES, 256))
    keep = jnp.broadcast_to(flags_ref[...].astype(F32), (LANES, 256))
    chain_t, keep_t = chain.T, keep.T
    bias_t = bias.T
    extra = []
    for half in range(2):
        cols = slice(half * LANES, (half + 1) * LANES)
        cross = jnp.where(chain_t != chain_ref[:, cols].astype(F32), offset, 0.0)
        extra.append(jnp.where(keep_t > 0.0, bias_t[:, cols] + cross, -1000000000.0))
    extra = jnp.concatenate(extra, axis=1)
    keep_k = keep_t[:, :DH].astype(BF16)
    lane3 = lanes((N, 8, LANES))

    for r in range(N):
        x = x_ref[r * 256 : (r + 1) * 256, :]
        scores = dot(x[:, DH : 2 * DH] * keep_k, x[:, :DH], NT) + extra
        exp_scores = jnp.exp(scores - jnp.max(scores, axis=0, keepdims=True))
        total = jnp.sum(exp_scores, axis=0, keepdims=True)
        attended = dot(x[:, 2 * DH : 3 * DH], exp_scores.astype(BF16), TN) / total
        both = jnp.concatenate([attended, attended, attended, attended], axis=0).T.reshape(N, 2, 8, LANES)
        chunk = jnp.where(lane3 < 64, both[:, 0], both[:, 1])
        chunk = jnp.where(lane3 % 64 < DH, chunk, ps_ref[:, r])
        out_ref[r * LANES : (r + 1) * LANES, :] = chunk.reshape(LANES, LANES).astype(BF16)


def mid(received, flags, chain, offset):
    return pl.pallas_call(
        mid_kernel,
        out_shape=jax.ShapeDtypeStruct((2048, LANES), BF16),
        in_specs=[SMEM] + [VMEM] * 3,
        out_specs=VMEM,
        scratch_shapes=[pltpu.VMEM((N, N, 8, LANES), F32)],
        compiler_params=pltpu.CompilerParams(vmem_limit_bytes=32 * 2**20),
        name="mid",
    )(offset, flags.reshape(1, 256), chain.reshape(1, 256), received)


def post_kernel(x_ref, homolog_ref, pair_ref, msa_ref, pn_ref, wg_ref, wf_ref, wtg_ref, wtf_ref, out_ref, pair_out_ref, t_ref):
    x = x_ref[...].astype(F32).reshape(HEADS, 32, 8, LANES)
    group = lanes((32, 8, LANES)) // DH
    attended = []
    for g in range(2):
        parts = [None, None]
        for hh in range(4):
            for u in range(2):
                moved = turn(x[g * 4 + hh], hh * DH - u * 64)
                parts[u] = moved if hh == 0 else jnp.where(group == hh, moved, parts[u])
        attended.append(jnp.stack(parts, axis=1).reshape(512, LANES))
    attended = jnp.concatenate(attended, axis=1)
    gated = (jax.nn.sigmoid(dot(msa_ref[...], wg_ref[...])) * attended).astype(BF16)
    out = homolog_ref[...].reshape(512, 256).astype(F32) + dot(gated, wf_ref[...])
    out_ref[...] = out.astype(BF16).reshape(32, 16, 256)

    t = x.reshape(256, 8, LANES)
    t = t[:LANES] + t[LANES:]
    t = t + turn(t, -16)
    t_ref[...] = t.reshape(1024, LANES)
    upper, lower = [], []
    for i8 in range(8):
        rows = t_ref[pl.ds(i8, LANES, stride=8), :].T
        upper.append(rows[32:48])
        lower.append(rows[96:112])
    product_norm = standardize(jnp.concatenate(upper + lower, axis=0)).astype(BF16)
    update = jax.nn.sigmoid(dot(pn_ref[...], wtg_ref[...])) * dot(product_norm, wtf_ref[...])
    pair_out = pair_ref[...].reshape(N * N, LANES).astype(F32) + update
    pair_out_ref[...] = pair_out.astype(BF16).reshape(N, N, LANES)


def post(received, homolog, pair, msa_norm, pair_norm, w_gate, w_final, w_tri_gate, w_tri_final):
    return pl.pallas_call(
        post_kernel,
        out_shape=(jax.ShapeDtypeStruct(homolog.shape, BF16), jax.ShapeDtypeStruct(pair.shape, BF16)),
        in_specs=[VMEM] * 9,
        out_specs=(VMEM, VMEM),
        scratch_shapes=[pltpu.VMEM((1024, LANES), F32)],
        compiler_params=pltpu.CompilerParams(vmem_limit_bytes=32 * 2**20),
        name="post",
    )(received, homolog, pair, msa_norm, pair_norm, w_gate, w_final, w_tri_gate, w_tri_final)


def exchange(chunks):
    return lax.all_to_all(chunks, AXES, split_axis=0, concat_axis=0, tiled=True)


def local(
    homolog_tensor,
    pairwise_tensor,
    genuine_amino_flags,
    polymer_identity,
    asking_weights,
    attend_sigmoid_weights,
    lookup_content_weights,
    attend_final_weights,
    pairwise_logit_weights,
    crosspolymer_offset,
    outgoing_link_weights,
    incoming_link_weights,
    trimult_sigmoid_weights,
    trimult_final_weights,
):
    send, msa_norm, pair_norm = pre(
        homolog_tensor,
        pairwise_tensor,
        genuine_amino_flags,
        asking_weights,
        lookup_content_weights,
        pairwise_logit_weights,
        outgoing_link_weights,
        incoming_link_weights,
    )
    back = mid(exchange(send), genuine_amino_flags, polymer_identity, crosspolymer_offset)
    return post(
        exchange(back),
        homolog_tensor,
        pairwise_tensor,
        msa_norm,
        pair_norm,
        attend_sigmoid_weights,
        attend_final_weights,
        trimult_sigmoid_weights,
        trimult_final_weights,
    )


def solution(mesh):
    block = P("row", "col", None)
    in_specs = (block, block) + (P(),) * 12
    return jax.shard_map(local, mesh=mesh, in_specs=in_specs, out_specs=(block, block), check_vma=False)
```

time: 125 us -> 92.8 us (0.74)
  blocking collectives: 26.2 us -> 74.2 us
  waiting for transfers between devices: 32 us -> 0 us
  local copies, waits for them, and re-layouts: 22.6 us -> 6.84 us
  starting transfers between devices: 15.7 us -> 0 us
  other arithmetic: 14 us -> 0 us
  matrix products: 13 us -> 0 us
  Pallas kernels: 0 us -> 10.6 us
    all_to_all x1 -> x2, blocking collectives: 26.2 us -> 74.2 us  [exchange(): return lax.all_to_all(chunks, AXES, split_axis=0, concat_axis=0, tiled=True)]
    all_to_all x1 -> x0, waiting for transfers between devices: 32 us -> none  [exchange(): return lax.all_to_all(chunks, AXES, split_axis=0, concat_axis=0, tiled=True)]
    all_to_all x1 -> x0, starting transfers between devices: 15.7 us -> none  [exchange(): return lax.all_to_all(chunks, AXES, split_axis=0, concat_axis=0, tiled=True)]
    dot_general x11 -> x0, matrix products: 13 us -> none  [the longest x8 9.74 us: dot(): return jnp.dot(a, b, preferred_element_type=F32)]
    pallas_call x0 -> x3, Pallas kernels: none -> 10.6 us  [the longest x1 5.83 us: mid(): pl.pallas_call(mid_kernel, out_shape=jax.ShapeDtypeStruct((2048, LANES),...]
    reshape x14 -> x0, local copies, waits for them, and re-layouts: 8.87 us -> none  [the longest x6 5.24 us: pre(): a.reshape(seqs, res, heads, dh)]
    convert_element_type x7 -> x0, local copies, waits for them, and re-layouts: 8.06 us -> none  [the longest x3 5.36 us: post(): attended.astype(F32)]
    unnamed x22 -> x31, local copies, waits for them, and re-layouts: 0.71 us -> 6.84 us
  transfers between devices with their start and end apart: 1 -> 0, of which waited for: 1 -> 0; matrix products, arithmetic and copies ran while one was open for 0% -> 0% of each run, Pallas kernels for 0% -> 0%
where the time goes in v2:
time: 92.8 us; the launch traced here: 92.4 us
  blocking collectives  74.2 us (80%)
  Pallas kernels  10.6 us (11%)
  local copies, waits for them, and re-layouts  6.84 us (7%)
    all_to_all x2, blocking collectives, exchange(): return lax.all_to_all(chunks, AXES, split_axis=0, concat_axis=0, tiled=True)  74.2 us
    unnamed x31, local copies, waits for them, and re-layouts  6.84 us
    pallas_call x1, Pallas kernels, mid(): pl.pallas_call(mid_kernel, out_shape=jax.ShapeDtypeStruct((2048, LANES),...  5.83 us
    pallas_call x1, Pallas kernels, pre(): pl.pallas_call(pre_kernel, out_shape=(jax.ShapeDtypeStruct((4096, LANES),...  3.2 us

profile of v2, /device:TPU:1, one launch (start us, length us, event | category | flops | bytes accessed | tf_op | source)
XLA Modules:
  0.0 92.4 jit_solution(3008197911913088614)
XLA Ops:
  0.6 0.0 copy-start.12
  0.6 0.8 copy.16.wb_ref
  1.4 0.0 copy-done.12
  1.4 0.0 copy-start
  1.5 0.9 %copy-done = bf16[32,16,256]{2,1,0:T(8,128)(2,1)S(1)} copy-done((bf16[32,16,256]{2,1,0:T(8,128)(2,1)S(1)}, bf16[32,16,256]{2,1,0:T(8,128)(2,1)}, u32[]{:S(2)}) %copy-start) | copy-done | bytes 262168
  2.4 0.0 copy-start.2
  2.4 0.9 %copy-done.2 = bf16[256,512]{1,0:T(8,128)(2,1)S(1)} copy-done((bf16[256,512]{1,0:T(8,128)(2,1)S(1)}, bf16[256,512]{1,0:T(8,128)(2,1)}, u32[]{:S(2)}) %copy-start.2) | copy-done | bytes 262168
  3.4 0.0 copy-start.3
  3.4 0.8 copy-done.3
  4.2 0.0 copy-start.7
  4.2 0.9 copy-done.7
  5.1 0.0 copy-start.8
  5.1 0.8 copy-done.8
  5.9 0.0 copy-start.9
  5.9 0.8 copy-done.9
  6.8 3.2 %pre.1 = (bf16[4096,128]{1,0:T(8,128)(2,1)S(1)}, bf16[512,256]{1,0:T(8,128)(2,1)S(1)}, bf16[256,128]{1,0:T(8,128)(2,1)S(1)}) custom-call(s32[256]{0:T(256)S(1)} %copy-done.12, bf16[32,16,256]{2,1,0:T(8,128)(2,1)S(1)} %copy-done, bf16[16,16,128]{2,1,0:T(8,128)(2,1)S(1)} %copy-done.3, bf16[256,256]{1,0:T(8,128)(2,1)S(1)} %copy-done.7, ...), custom_call_target="tpu_custom_call" | custom-call | tf_op jit(solution)/shard_map/pre/pallas_call | solution.py:76
  10.0 48.1 %all_to_all.22 = bf16[256,16,128]{2,1,0:T(8,128)(2,1)S(1)} all-to-all(bf16[256,16,128]{2,1,0:T(8,128)(2,1)S(1)} %bitcast.9), channel_id=1, replica_groups=mesh['row'=16,'col'=16] {'row','col'}, dimensions={0} | all-to-all | bytes 2097152 | tf_op jit(solution)/shard_map/all_to_all | solution.py:215
  58.0 0.0 copy-start.13
  58.1 0.0 copy-start.14
  58.1 0.7 copy-done.13
  58.7 0.0 copy-done.14
  58.7 5.8 %mid.1 = bf16[2048,128]{1,0:T(8,128)(2,1)S(1)} custom-call(f32[8]{0:T(128)S(1)} %copy-done.14, s32[1,256]{1,0:T(1,128)S(1)} %bitcast.10, s32[1,256]{1,0:T(1,128)S(1)} %bitcast.11, bf16[4096,128]{1,0:T(8,128)(2,1)S(1)} %bitcast.6), custom_call_target="tpu_custom_call" | custom-call | tf_op jit(solution)/shard_map/mid/pallas_call | solution.py:160
  64.6 0.0 copy-start.1
  64.6 0.0 copy-start.4
  64.6 0.0 copy-start.5
  64.6 0.0 copy-start.6
  64.6 0.0 copy-start.10
  64.6 0.0 copy-start.11
  64.6 26.2 %all_to_all.23 = bf16[256,8,128]{2,1,0:T(8,128)(2,1)S(1)} all-to-all(bf16[256,8,128]{2,1,0:T(8,128)(2,1)S(1)} %bitcast.8), channel_id=1, replica_groups=mesh['row'=16,'col'=16] {'row','col'}, dimensions={0} | all-to-all | bytes 1048576 | tf_op jit(solution)/shard_map/all_to_all | solution.py:215
  90.8 0.0 copy-done.1
  90.8 0.0 copy-done.4
  90.8 0.0 copy-done.5
  90.8 0.0 copy-done.6
  90.8 0.0 copy-done.10
  90.8 0.0 copy-done.11
  90.9 1.6 %post.1 = (bf16[32,16,256]{2,1,0:T(8,128)(2,1)}, bf16[16,16,128]{2,1,0:T(8,128)(2,1)}) custom-call(bf16[2048,128]{1,0:T(8,128)(2,1)S(1)} %bitcast.7, bf16[32,16,256]{2,1,0:T(8,128)(2,1)S(1)} %copy-done.1, bf16[16,16,128]{2,1,0:T(8,128)(2,1)S(1)} %copy-done.4, bf16[512,256]{1,0:T(8,128)(2,1)S(1)} %get-tuple-element.6.msa_ref, ...), custom_call_target="tpu_custom_call" | custom-call | tf_op jit(solution)/shard_map/post/pallas_call | solution.py:203
Async XLA Ops:
  0.6 0.8 copy-start.12
  1.4 1.0 %copy-start = (bf16[32,16,256]{2,1,0:T(8,128)(2,1)S(1)}, bf16[32,16,256]{2,1,0:T(8,128)(2,1)}, u32[]{:S(2)}) copy-start(bf16[32,16,256]{2,1,0:T(8,128)(2,1)} %homolog_ref.1) | copy-start | bytes 786436
  2.4 0.9 %copy-start.2 = (bf16[256,512]{1,0:T(8,128)(2,1)S(1)}, bf16[256,512]{1,0:T(8,128)(2,1)}, u32[]{:S(2)}) copy-start(bf16[256,512]{1,0:T(8,128)(2,1)} %wkv_ref.1) | copy-start | bytes 786436
  3.4 0.8 copy-start.3
  4.2 0.9 copy-start.7
  5.1 0.8 copy-start.8
  5.9 0.8 copy-start.9
  58.0 0.7 copy-start.13
  58.1 0.7 copy-start.14
  64.6 26.2 %copy-start.1 = (bf16[32,16,256]{2,1,0:T(8,128)(2,1)S(1)}, bf16[32,16,256]{2,1,0:T(8,128)(2,1)}, u32[]{:S(2)}) copy-start(bf16[32,16,256]{2,1,0:T(8,128)(2,1)} %homolog_ref.1) | copy-start | bytes 786436
  64.6 26.2 %copy-start.4 = (bf16[16,16,128]{2,1,0:T(8,128)(2,1)S(1)}, bf16[16,16,128]{2,1,0:T(8,128)(2,1)}, u32[]{:S(2)}) copy-start(bf16[16,16,128]{2,1,0:T(8,128)(2,1)} %pair_ref.3) | copy-start | bytes 196612
  64.6 26.2 %copy-start.5 = (bf16[256,256]{1,0:T(8,128)(2,1)S(1)}, bf16[256,256]{1,0:T(8,128)(2,1)}, u32[]{:S(2)}) copy-start(bf16[256,256]{1,0:T(8,128)(2,1)} %wg_ref.1) | copy-start | bytes 393220
  64.6 26.2 %copy-start.6 = (bf16[256,256]{1,0:T(8,128)(2,1)S(1)}, bf16[256,256]{1,0:T(8,128)(2,1)}, u32[]{:S(2)}) copy-start(bf16[256,256]{1,0:T(8,128)(2,1)} %wf_ref.1) | copy-start | bytes 393220
  64.6 26.2 %copy-start.10 = (bf16[128,128]{1,0:T(8,128)(2,1)S(1)}, bf16[128,128]{1,0:T(8,128)(2,1)}, u32[]{:S(2)}) copy-start(bf16[128,128]{1,0:T(8,128)(2,1)} %wtg_ref.1) | copy-start | bytes 98308
  64.6 26.2 %copy-start.11 = (bf16[128,128]{1,0:T(8,128)(2,1)S(1)}, bf16[128,128]{1,0:T(8,128)(2,1)}, u32[]{:S(2)}) copy-start(bf16[128,128]{1,0:T(8,128)(2,1)} %wtf_ref.1) | copy-start | bytes 98308

commit v3 on v2

--- a/solution.py
+++ b/solution.py
@@ -13,7 +13,7 @@
 DH = 32
 LANES = 128
 VMEM = pl.BlockSpec(memory_space=pltpu.VMEM)
-SMEM = pl.BlockSpec(memory_space=pltpu.SMEM)
+HBM = pl.BlockSpec(memory_space=pltpu.HBM)
 NT = (((1,), (1,)), ((), ()))
 TN = (((0,), (0,)), ((), ()))
 
@@ -38,8 +38,37 @@
     return x if by == 0 else pltpu.roll(x, by, x.ndim - 1)
 
 
-def pre_kernel(flags_ref, x_ref, pair_ref, wq_ref, wkv_ref, wb_ref, wo_ref, wi_ref, send_ref, msa_ref, pn_ref, tri_ref, bias_ref):
+def fetch(pairs, sems):
+    copies = [pltpu.make_async_copy(source, target, sems.at[i]) for i, (source, target) in enumerate(pairs)]
+    for copy in copies:
+        copy.start()
+    return copies
+
+
+def pre_kernel(
+    pair_hbm, wo_hbm, wi_hbm, flags_hbm, wb_hbm, x_hbm, wq_hbm, wkv_hbm, offset_hbm, flags2_hbm, chain_hbm,
+    send_ref, msa_ref, pn_ref, aux_ref,
+    pair_ref, wo_ref, wi_ref, flags_ref, wb_ref, x_ref, wq_ref, wkv_ref, offset_ref, flags2_ref, chain_ref, tri_ref, bias_ref, sems,
+):
     row = lax.axis_index("row")
+    copies = fetch(
+        (
+            (pair_hbm, pair_ref),
+            (wo_hbm, wo_ref),
+            (wi_hbm, wi_ref),
+            (flags_hbm, flags_ref),
+            (wb_hbm, wb_ref),
+            (x_hbm, x_ref),
+            (wq_hbm, wq_ref),
+            (wkv_hbm, wkv_ref),
+            (offset_hbm, offset_ref),
+            (flags2_hbm, flags2_ref),
+            (chain_hbm, chain_ref),
+        ),
+        sems,
+    )
+    for copy in copies[:4]:
+        copy.wait()
     pair_norm = standardize(pair_ref[...].reshape(N * N, LANES)).astype(BF16)
     pn_ref[...] = pair_norm
     for w_ref, first in ((wo_ref, 0), (wi_ref, 8)):
@@ -50,46 +79,65 @@
             flag = flags_ref[row * N + k].astype(F32)
             part = turn(edge[:, half * LANES : (half + 1) * LANES], 112 - k8 * 16) * flag
             tri_ref[pl.ds(half * 2048 + first + k8, LANES, stride=16), :] = part
-    wb = jnp.concatenate([wb_ref[...].astype(F32), jnp.zeros((LANES, LANES - HEADS), F32)], axis=1).T
-    bias = dot(wb[:HEADS].astype(BF16), pair_norm, NT)
+    copies[4].wait()
+    bias = dot(wb_ref[...], pair_norm, NT)
     for i in range(N):
         half, i8 = i // 8, i % 8
         bias_ref[pl.ds(i, HEADS, stride=16), :] = turn(bias[:, half * LANES : (half + 1) * LANES], 96 - i8 * 16)
 
+    for copy in copies[5:]:
+        copy.wait()
     msa_norm = standardize(x_ref[...].reshape(512, 256)).astype(BF16)
     msa_ref[...] = msa_norm
     lane = lanes((512, LANES))
-    for h in range(HEADS):
-        cut = slice(h * DH, (h + 1) * DH)
-        cut_v = slice(256 + h * DH, 256 + (h + 1) * DH)
-        weight = jnp.concatenate([wq_ref[:, cut], wkv_ref[:, cut], wkv_ref[:, cut_v], wq_ref[:, cut]], axis=1)
-        y = dot(msa_norm, weight)
-        y = jnp.where(lane < DH, y * DH**-0.5, y)
-        bias_h = bias_ref[h * 16 : (h + 1) * 16, :]
-        bias_h = jnp.broadcast_to(bias_h[None], (32, 16, LANES)).reshape(512, LANES)
-        tri = tri_ref[h * 512 : (h + 1) * 512, :]
-        out = jnp.where(lane < 96, y, jnp.where(lane < 112, bias_h, tri))
-        send_ref[h * 512 : (h + 1) * 512, :] = out.astype(BF16)
-
-
-def pre(homolog, pair, flags, w_q, w_kv, w_bias, w_out, w_in):
+    for h in range(0, HEADS, 2):
+        parts = []
+        for head in (h, h + 1):
+            cut = slice(head * DH, (head + 1) * DH)
+            cut_v = slice(256 + head * DH, 256 + (head + 1) * DH)
+            parts += [wq_ref[:, cut], wkv_ref[:, cut], wkv_ref[:, cut_v], wq_ref[:, cut]]
+        both = dot(msa_norm, jnp.concatenate(parts, axis=1))
+        for head in (h, h + 1):
+            y = both[:, (head - h) * LANES : (head - h + 1) * LANES]
+            y = jnp.where(lane < DH, y * DH**-0.5, y)
+            bias_h = bias_ref[head * 16 : (head + 1) * 16, :]
+            bias_h = jnp.broadcast_to(bias_h[None], (32, 16, LANES)).reshape(512, LANES)
+            tri = tri_ref[head * 512 : (head + 1) * 512, :]
+            out = jnp.where(lane < 96, y, jnp.where(lane < 112, bias_h, tri))
+            send_ref[head * 512 : (head + 1) * 512, :] = out.astype(BF16)
+    aux_ref[0:1, :] = flags2_ref[...].astype(F32)
+    aux_ref[1:2, :] = chain_ref[...].astype(F32)
+    aux_ref[2:3, :] = jnp.full((1, 256), offset_ref[row // 2], F32)
+
+
+def in_hbm(*arrays):
+    return [pltpu.with_memory_space_constraint(a, pltpu.HBM) for a in arrays]
+
+
+def scratch_like(*arrays):
+    return [(pltpu.SMEM if a.ndim == 1 else pltpu.VMEM)(a.shape, a.dtype) for a in arrays]
+
+
+def pre(homolog, pair, flags, chain, offset, w_q, w_kv, w_bias, w_out, w_in):
+    operands = (pair, w_out, w_in, flags, w_bias.T, homolog, w_q, w_kv, offset, flags.reshape(1, 256), chain.reshape(1, 256))
     return pl.pallas_call(
         pre_kernel,
         out_shape=(
             jax.ShapeDtypeStruct((4096, LANES), BF16),
             jax.ShapeDtypeStruct((512, 256), BF16),
             jax.ShapeDtypeStruct((256, LANES), BF16),
+            jax.ShapeDtypeStruct((8, 256), F32),
         ),
-        in_specs=[SMEM] + [VMEM] * 7,
-        out_specs=(VMEM, VMEM, VMEM),
-        scratch_shapes=[pltpu.VMEM((4096, LANES), F32), pltpu.VMEM((LANES, LANES), F32)],
+        in_specs=[HBM] * 11,
+        out_specs=(VMEM, VMEM, VMEM, VMEM),
+        scratch_shapes=scratch_like(*operands)
+        + [pltpu.VMEM((4096, LANES), F32), pltpu.VMEM((LANES, LANES), F32), pltpu.SemaphoreType.DMA((11,))],
         compiler_params=pltpu.CompilerParams(vmem_limit_bytes=32 * 2**20),
         name="pre",
-    )(flags, homolog, pair, w_q, w_kv, w_bias, w_out, w_in)
-
-
-def mid_kernel(offset_ref, flags_ref, chain_ref, x_ref, out_ref, ps_ref):
-    offset = offset_ref[lax.axis_index("row") // 2]
+    )(*in_hbm(*operands))
+
+
+def mid_kernel(aux_ref, x_ref, out_ref, ps_ref):
     wide = (256, LANES)
     slot = lanes(wide) // 16
     bias_cols, tri_cols = [], []
@@ -131,14 +179,14 @@
                 for c8 in firsts:
                     ps_ref[half * 8 + c8] = turn(merged, 32 - c8 * 16).reshape(N, 8, LANES)
 
-    chain = jnp.broadcast_to(chain_ref[...].astype(F32), (LANES, 256))
-    keep = jnp.broadcast_to(flags_ref[...].astype(F32), (LANES, 256))
+    chain = jnp.broadcast_to(aux_ref[1:2, :], (LANES, 256))
+    keep = jnp.broadcast_to(aux_ref[0:1, :], (LANES, 256))
     chain_t, keep_t = chain.T, keep.T
     bias_t = bias.T
     extra = []
     for half in range(2):
         cols = slice(half * LANES, (half + 1) * LANES)
-        cross = jnp.where(chain_t != chain_ref[:, cols].astype(F32), offset, 0.0)
+        cross = jnp.where(chain_t != aux_ref[1:2, cols], aux_ref[2:3, cols], 0.0)
         extra.append(jnp.where(keep_t > 0.0, bias_t[:, cols] + cross, -1000000000.0))
     extra = jnp.concatenate(extra, axis=1)
     keep_k = keep_t[:, :DH].astype(BF16)
@@ -156,16 +204,16 @@
         out_ref[r * LANES : (r + 1) * LANES, :] = chunk.reshape(LANES, LANES).astype(BF16)
 
 
-def mid(received, flags, chain, offset):
+def mid(received, aux):
     return pl.pallas_call(
         mid_kernel,
         out_shape=jax.ShapeDtypeStruct((2048, LANES), BF16),
-        in_specs=[SMEM] + [VMEM] * 3,
+        in_specs=[VMEM] * 2,
         out_specs=VMEM,
         scratch_shapes=[pltpu.VMEM((N, N, 8, LANES), F32)],
         compiler_params=pltpu.CompilerParams(vmem_limit_bytes=32 * 2**20),
         name="mid",
-    )(offset, flags.reshape(1, 256), chain.reshape(1, 256), received)
+    )(aux, received)
 
 
 def post_kernel(x_ref, homolog_ref, pair_ref, msa_ref, pn_ref, wg_ref, wf_ref, wtg_ref, wtf_ref, out_ref, pair_out_ref, t_ref):
@@ -231,17 +279,19 @@
     trimult_sigmoid_weights,
     trimult_final_weights,
 ):
-    send, msa_norm, pair_norm = pre(
+    send, msa_norm, pair_norm, aux = pre(
         homolog_tensor,
         pairwise_tensor,
         genuine_amino_flags,
+        polymer_identity,
+        crosspolymer_offset,
         asking_weights,
         lookup_content_weights,
         pairwise_logit_weights,
         outgoing_link_weights,
         incoming_link_weights,
     )
-    back = mid(exchange(send), genuine_amino_flags, polymer_identity, crosspolymer_offset)
+    back = mid(exchange(send), aux)
     return post(
         exchange(back),
         homolog_tensor,

time: 92.8 us -> 85.5 us (0.921)
  local copies, waits for them, and re-layouts: 6.84 us -> 0.04 us
    unnamed x31 -> x12, local copies, waits for them, and re-layouts: 6.84 us -> 0.04 us
where the time goes in v3:
time: 85.5 us; the launch traced here: 85.4 us
  blocking collectives  74.2 us (87%)
  Pallas kernels  10.4 us (12%)
    all_to_all x2, blocking collectives, exchange(): return lax.all_to_all(chunks, AXES, split_axis=0, concat_axis=0, tiled=True)  74.2 us
    pallas_call x1, Pallas kernels, mid(): pl.pallas_call(mid_kernel, out_shape=jax.ShapeDtypeStruct((2048, LANES),...  5.3 us
    pallas_call x1, Pallas kernels, pre(): pl.pallas_call(pre_kernel, out_shape=(jax.ShapeDtypeStruct((4096, LANES),...  3.51 us

profile of v3, /device:TPU:1, one launch (start us, length us, event | category | flops | bytes accessed | tf_op | source)
XLA Modules:
  0.0 85.4 jit_solution(1959472327452702795)
XLA Ops:
  0.6 3.5 %pre.1 = (bf16[4096,128]{1,0:T(8,128)(2,1)S(1)}, bf16[512,256]{1,0:T(8,128)(2,1)S(1)}, bf16[256,128]{1,0:T(8,128)(2,1)S(1)}, f32[8,256]{1,0:T(8,128)S(1)}) custom-call(bf16[16,16,128]{2,1,0:T(8,128)(2,1)} %pair_ref.1, bf16[128,256]{1,0:T(8,128)(2,1)} %wo_hbm.1, bf16[128,256]{1,0:T(8,128)(2,1)} %wi_hbm.1, s32[256]{0:T(256)} %flags_hbm.1, ...), custom_call_target="tpu_custom_call" | custom-call | tf_op jit(solution)/shard_map/pre/pallas_call | solution.py:123
  4.2 48.1 %all_to_all.22 = bf16[256,16,128]{2,1,0:T(8,128)(2,1)S(1)} all-to-all(bf16[256,16,128]{2,1,0:T(8,128)(2,1)S(1)} %bitcast.10), channel_id=1, replica_groups=mesh['row'=16,'col'=16] {'row','col'}, dimensions={0} | all-to-all | bytes 2097152 | tf_op jit(solution)/shard_map/all_to_all | solution.py:263
  52.2 5.3 %mid.1 = bf16[2048,128]{1,0:T(8,128)(2,1)S(1)} custom-call(f32[8,256]{1,0:T(8,128)S(1)} %get-tuple-element.6.aux_ref, bf16[4096,128]{1,0:T(8,128)(2,1)S(1)} %bitcast.7), custom_call_target="tpu_custom_call" | custom-call | tf_op jit(solution)/shard_map/mid/pallas_call | solution.py:208
  57.5 0.0 copy-start
  57.5 0.0 copy-start.1
  57.6 0.0 copy-start.2
  57.6 0.0 copy-start.3
  57.6 0.0 copy-start.4
  57.6 0.0 copy-start.5
  57.6 26.2 %all_to_all.23 = bf16[256,8,128]{2,1,0:T(8,128)(2,1)S(1)} all-to-all(bf16[256,8,128]{2,1,0:T(8,128)(2,1)S(1)} %bitcast.9), channel_id=1, replica_groups=mesh['row'=16,'col'=16] {'row','col'}, dimensions={0} | all-to-all | bytes 1048576 | tf_op jit(solution)/shard_map/all_to_all | solution.py:263
  83.8 0.0 copy-done
  83.8 0.0 copy-done.1
  83.8 0.0 copy-done.2
  83.8 0.0 copy-done.3
  83.8 0.0 copy-done.4
  83.8 0.0 copy-done.5
  83.8 1.6 %post.1 = (bf16[32,16,256]{2,1,0:T(8,128)(2,1)}, bf16[16,16,128]{2,1,0:T(8,128)(2,1)}) custom-call(bf16[2048,128]{1,0:T(8,128)(2,1)S(1)} %bitcast.8, bf16[32,16,256]{2,1,0:T(8,128)(2,1)S(1)} %copy-done, bf16[16,16,128]{2,1,0:T(8,128)(2,1)S(1)} %copy-done.1, bf16[512,256]{1,0:T(8,128)(2,1)S(1)} %get-tuple-element.8.msa_ref, ...), custom_call_target="tpu_custom_call" | custom-call | tf_op jit(solution)/shard_map/post/pallas_call | solution.py:251
Async XLA Ops:
  57.5 26.2 %copy-start = (bf16[32,16,256]{2,1,0:T(8,128)(2,1)S(1)}, bf16[32,16,256]{2,1,0:T(8,128)(2,1)}, u32[]{:S(2)}) copy-start(bf16[32,16,256]{2,1,0:T(8,128)(2,1)} %homolog_ref.1) | copy-start | bytes 786436
  57.5 26.2 %copy-start.1 = (bf16[16,16,128]{2,1,0:T(8,128)(2,1)S(1)}, bf16[16,16,128]{2,1,0:T(8,128)(2,1)}, u32[]{:S(2)}) copy-start(bf16[16,16,128]{2,1,0:T(8,128)(2,1)} %pair_ref.1) | copy-start | bytes 196612
  57.6 26.2 %copy-start.2 = (bf16[256,256]{1,0:T(8,128)(2,1)S(1)}, bf16[256,256]{1,0:T(8,128)(2,1)}, u32[]{:S(2)}) copy-start(bf16[256,256]{1,0:T(8,128)(2,1)} %wg_ref.1) | copy-start | bytes 393220
  57.6 26.2 %copy-start.3 = (bf16[256,256]{1,0:T(8,128)(2,1)S(1)}, bf16[256,256]{1,0:T(8,128)(2,1)}, u32[]{:S(2)}) copy-start(bf16[256,256]{1,0:T(8,128)(2,1)} %wf_ref.1) | copy-start | bytes 393220
  57.6 26.2 %copy-start.4 = (bf16[128,128]{1,0:T(8,128)(2,1)S(1)}, bf16[128,128]{1,0:T(8,128)(2,1)}, u32[]{:S(2)}) copy-start(bf16[128,128]{1,0:T(8,128)(2,1)} %wtg_ref.1) | copy-start | bytes 98308
  57.6 26.2 %copy-start.5 = (bf16[128,128]{1,0:T(8,128)(2,1)S(1)}, bf16[128,128]{1,0:T(8,128)(2,1)}, u32[]{:S(2)}) copy-start(bf16[128,128]{1,0:T(8,128)(2,1)} %wtf_ref.1) | copy-start | bytes 98308

commit v4 on v3

--- a/solution.py
+++ b/solution.py
@@ -67,8 +67,10 @@
         ),
         sems,
     )
-    for copy in copies[:4]:
+    for copy in copies:
         copy.wait()
+    msa_norm = standardize(x_ref[...].reshape(512, 256)).astype(BF16)
+    msa_ref[...] = msa_norm
     pair_norm = standardize(pair_ref[...].reshape(N * N, LANES)).astype(BF16)
     pn_ref[...] = pair_norm
     for w_ref, first in ((wo_ref, 0), (wi_ref, 8)):
@@ -79,16 +81,11 @@
             flag = flags_ref[row * N + k].astype(F32)
             part = turn(edge[:, half * LANES : (half + 1) * LANES], 112 - k8 * 16) * flag
             tri_ref[pl.ds(half * 2048 + first + k8, LANES, stride=16), :] = part
-    copies[4].wait()
     bias = dot(wb_ref[...], pair_norm, NT)
     for i in range(N):
         half, i8 = i // 8, i % 8
         bias_ref[pl.ds(i, HEADS, stride=16), :] = turn(bias[:, half * LANES : (half + 1) * LANES], 96 - i8 * 16)
 
-    for copy in copies[5:]:
-        copy.wait()
-    msa_norm = standardize(x_ref[...].reshape(512, 256)).astype(BF16)
-    msa_ref[...] = msa_norm
     lane = lanes((512, LANES))
     for h in range(0, HEADS, 2):
         parts = []
@@ -192,16 +189,32 @@
     keep_k = keep_t[:, :DH].astype(BF16)
     lane3 = lanes((N, 8, LANES))
 
-    for r in range(N):
-        x = x_ref[r * 256 : (r + 1) * 256, :]
-        scores = dot(x[:, DH : 2 * DH] * keep_k, x[:, :DH], NT) + extra
-        exp_scores = jnp.exp(scores - jnp.max(scores, axis=0, keepdims=True))
-        total = jnp.sum(exp_scores, axis=0, keepdims=True)
-        attended = dot(x[:, 2 * DH : 3 * DH], exp_scores.astype(BF16), TN) / total
+
+    def finish(r, attended):
         both = jnp.concatenate([attended, attended, attended, attended], axis=0).T.reshape(N, 2, 8, LANES)
         chunk = jnp.where(lane3 < 64, both[:, 0], both[:, 1])
         chunk = jnp.where(lane3 % 64 < DH, chunk, ps_ref[:, r])
         out_ref[r * LANES : (r + 1) * LANES, :] = chunk.reshape(LANES, LANES).astype(BF16)
+
+    def scores_of(r):
+        x = x_ref[r * 256 : (r + 1) * 256, :]
+        return dot(x[:, DH : 2 * DH] * keep_k, x[:, :DH], NT)
+
+    def attend(r, exp_scores, total):
+        return dot(x_ref[r * 256 : (r + 1) * 256, :][:, 2 * DH : 3 * DH], exp_scores, TN) / total
+
+    coming = scores_of(0)
+    prev = None
+    for r in range(N):
+        scores = coming + extra
+        if r + 1 < N:
+            coming = scores_of(r + 1)
+        exp_scores = jnp.exp(scores - jnp.max(scores, axis=0, keepdims=True))
+        total = jnp.sum(exp_scores, axis=0, keepdims=True)
+        if prev is not None:
+            finish(r - 1, attend(r - 1, *prev))
+        prev = (exp_scores.astype(BF16), total)
+    finish(N - 1, attend(N - 1, *prev))
 
 
 def mid(received, aux):

time: 85.5 us -> 84 us (0.982)
  Pallas kernels: 10.4 us -> 8.81 us
    pallas_call x1, Pallas kernels: 5.3 us -> 3.83 us  [mid(): pl.pallas_call(mid_kernel, out_shape=jax.ShapeDtypeStruct((2048, LANES),...]
where the time goes in v4:
time: 84 us; the launch traced here: 83.8 us
  blocking collectives  74.2 us (88%)
  Pallas kernels  8.81 us (10%)
    all_to_all x2, blocking collectives, exchange(): return lax.all_to_all(chunks, AXES, split_axis=0, concat_axis=0, tiled=True)  74.2 us
    pallas_call x1, Pallas kernels, mid(): pl.pallas_call(mid_kernel, out_shape=jax.ShapeDtypeStruct((2048, LANES),...  3.83 us
    pallas_call x1, Pallas kernels, pre(): pl.pallas_call(pre_kernel, out_shape=(jax.ShapeDtypeStruct((4096, LANES),...  3.4 us

profile of v4, /device:TPU:1, one launch (start us, length us, event | category | flops | bytes accessed | tf_op | source)
XLA Modules:
  0.0 83.8 jit_solution(3056425682405274752)
XLA Ops:
  0.6 3.4 %pre.1 = (bf16[4096,128]{1,0:T(8,128)(2,1)S(1)}, bf16[512,256]{1,0:T(8,128)(2,1)S(1)}, bf16[256,128]{1,0:T(8,128)(2,1)S(1)}, f32[8,256]{1,0:T(8,128)S(1)}) custom-call(bf16[16,16,128]{2,1,0:T(8,128)(2,1)} %pair_ref.1, bf16[128,256]{1,0:T(8,128)(2,1)} %wo_hbm.1, bf16[128,256]{1,0:T(8,128)(2,1)} %wi_hbm.1, s32[256]{0:T(256)} %flags_hbm.1, ...), custom_call_target="tpu_custom_call" | custom-call | tf_op jit(solution)/shard_map/pre/pallas_call | solution.py:120
  4.0 48.1 %all_to_all.22 = bf16[256,16,128]{2,1,0:T(8,128)(2,1)S(1)} all-to-all(bf16[256,16,128]{2,1,0:T(8,128)(2,1)S(1)} %bitcast.10), channel_id=1, replica_groups=mesh['row'=16,'col'=16] {'row','col'}, dimensions={0} | all-to-all | bytes 2097152 | tf_op jit(solution)/shard_map/all_to_all | solution.py:276
  52.1 3.8 %mid.1 = bf16[2048,128]{1,0:T(8,128)(2,1)S(1)} custom-call(f32[8,256]{1,0:T(8,128)S(1)} %get-tuple-element.6.aux_ref, bf16[4096,128]{1,0:T(8,128)(2,1)S(1)} %bitcast.7), custom_call_target="tpu_custom_call" | custom-call | tf_op jit(solution)/shard_map/mid/pallas_call | solution.py:221
  55.9 0.0 copy-start
  56.0 0.0 copy-start.1
  56.0 0.0 copy-start.2
  56.0 0.0 copy-start.3
  56.0 0.0 copy-start.4
  56.0 0.0 copy-start.5
  56.0 26.2 %all_to_all.23 = bf16[256,8,128]{2,1,0:T(8,128)(2,1)S(1)} all-to-all(bf16[256,8,128]{2,1,0:T(8,128)(2,1)S(1)} %bitcast.9), channel_id=1, replica_groups=mesh['row'=16,'col'=16] {'row','col'}, dimensions={0} | all-to-all | bytes 1048576 | tf_op jit(solution)/shard_map/all_to_all | solution.py:276
  82.2 0.0 copy-done
  82.2 0.0 copy-done.1
  82.2 0.0 copy-done.2
  82.2 0.0 copy-done.3
  82.2 0.0 copy-done.4
  82.2 0.0 copy-done.5
  82.2 1.6 %post.1 = (bf16[32,16,256]{2,1,0:T(8,128)(2,1)}, bf16[16,16,128]{2,1,0:T(8,128)(2,1)}) custom-call(bf16[2048,128]{1,0:T(8,128)(2,1)S(1)} %bitcast.8, bf16[32,16,256]{2,1,0:T(8,128)(2,1)S(1)} %copy-done, bf16[16,16,128]{2,1,0:T(8,128)(2,1)S(1)} %copy-done.1, bf16[512,256]{1,0:T(8,128)(2,1)S(1)} %get-tuple-element.8.msa_ref, ...), custom_call_target="tpu_custom_call" | custom-call | tf_op jit(solution)/shard_map/post/pallas_call | solution.py:264
Async XLA Ops:
  55.9 26.2 %copy-start = (bf16[32,16,256]{2,1,0:T(8,128)(2,1)S(1)}, bf16[32,16,256]{2,1,0:T(8,128)(2,1)}, u32[]{:S(2)}) copy-start(bf16[32,16,256]{2,1,0:T(8,128)(2,1)} %homolog_ref.1) | copy-start | bytes 786436
  56.0 26.2 %copy-start.1 = (bf16[16,16,128]{2,1,0:T(8,128)(2,1)S(1)}, bf16[16,16,128]{2,1,0:T(8,128)(2,1)}, u32[]{:S(2)}) copy-start(bf16[16,16,128]{2,1,0:T(8,128)(2,1)} %pair_ref.1) | copy-start | bytes 196612
  56.0 26.2 %copy-start.2 = (bf16[256,256]{1,0:T(8,128)(2,1)S(1)}, bf16[256,256]{1,0:T(8,128)(2,1)}, u32[]{:S(2)}) copy-start(bf16[256,256]{1,0:T(8,128)(2,1)} %wg_ref.1) | copy-start | bytes 393220
  56.0 26.2 %copy-start.3 = (bf16[256,256]{1,0:T(8,128)(2,1)S(1)}, bf16[256,256]{1,0:T(8,128)(2,1)}, u32[]{:S(2)}) copy-start(bf16[256,256]{1,0:T(8,128)(2,1)} %wf_ref.1) | copy-start | bytes 393220
  56.0 26.2 %copy-start.4 = (bf16[128,128]{1,0:T(8,128)(2,1)S(1)}, bf16[128,128]{1,0:T(8,128)(2,1)}, u32[]{:S(2)}) copy-start(bf16[128,128]{1,0:T(8,128)(2,1)} %wtg_ref.1) | copy-start | bytes 98308
  56.0 26.2 %copy-start.5 = (bf16[128,128]{1,0:T(8,128)(2,1)S(1)}, bf16[128,128]{1,0:T(8,128)(2,1)}, u32[]{:S(2)}) copy-start(bf16[128,128]{1,0:T(8,128)(2,1)} %wtf_ref.1) | copy-start | bytes 98308

commit v5 on v4

--- a/solution.py
+++ b/solution.py
@@ -50,15 +50,15 @@
     send_ref, msa_ref, pn_ref, aux_ref,
     pair_ref, wo_ref, wi_ref, flags_ref, wb_ref, x_ref, wq_ref, wkv_ref, offset_ref, flags2_ref, chain_ref, tri_ref, bias_ref, sems,
 ):
-    row = lax.axis_index("row")
+    row, col = lax.axis_index("row"), lax.axis_index("col")
     copies = fetch(
         (
+            (x_hbm, x_ref),
             (pair_hbm, pair_ref),
             (wo_hbm, wo_ref),
             (wi_hbm, wi_ref),
             (flags_hbm, flags_ref),
             (wb_hbm, wb_ref),
-            (x_hbm, x_ref),
             (wq_hbm, wq_ref),
             (wkv_hbm, wkv_ref),
             (offset_hbm, offset_ref),
@@ -67,10 +67,11 @@
         ),
         sems,
     )
-    for copy in copies:
-        copy.wait()
+    copies[0].wait()
     msa_norm = standardize(x_ref[...].reshape(512, 256)).astype(BF16)
     msa_ref[...] = msa_norm
+    for copy in copies[1:]:
+        copy.wait()
     pair_norm = standardize(pair_ref[...].reshape(N * N, LANES)).astype(BF16)
     pn_ref[...] = pair_norm
     for w_ref, first in ((wo_ref, 0), (wi_ref, 8)):
@@ -87,6 +88,13 @@
         bias_ref[pl.ds(i, HEADS, stride=16), :] = turn(bias[:, half * LANES : (half + 1) * LANES], 96 - i8 * 16)
 
     lane = lanes((512, LANES))
+    tile_row = lax.broadcasted_iota(jnp.int32, (N, LANES), 0)
+    keep = jnp.ones((N, LANES), F32)
+    for res in range(N):
+        keep = jnp.where(tile_row == res, flags_ref[col * N + res].astype(F32), keep)
+    tile_lane = lanes((N, LANES))
+    factor = jnp.where(tile_lane < DH, DH**-0.5, jnp.where(tile_lane < 2 * DH, keep, 1.0))
+    factor = jnp.broadcast_to(factor[None], (32, N, LANES)).reshape(512, LANES)
     for h in range(0, HEADS, 2):
         parts = []
         for head in (h, h + 1):
@@ -96,11 +104,10 @@
         both = dot(msa_norm, jnp.concatenate(parts, axis=1))
         for head in (h, h + 1):
             y = both[:, (head - h) * LANES : (head - h + 1) * LANES]
-            y = jnp.where(lane < DH, y * DH**-0.5, y)
             bias_h = bias_ref[head * 16 : (head + 1) * 16, :]
             bias_h = jnp.broadcast_to(bias_h[None], (32, 16, LANES)).reshape(512, LANES)
             tri = tri_ref[head * 512 : (head + 1) * 512, :]
-            out = jnp.where(lane < 96, y, jnp.where(lane < 112, bias_h, tri))
+            out = jnp.where(lane < 96, y * factor, jnp.where(lane < 112, bias_h, tri))
             send_ref[head * 512 : (head + 1) * 512, :] = out.astype(BF16)
     aux_ref[0:1, :] = flags2_ref[...].astype(F32)
     aux_ref[1:2, :] = chain_ref[...].astype(F32)
@@ -186,7 +193,6 @@
         cross = jnp.where(chain_t != aux_ref[1:2, cols], aux_ref[2:3, cols], 0.0)
         extra.append(jnp.where(keep_t > 0.0, bias_t[:, cols] + cross, -1000000000.0))
     extra = jnp.concatenate(extra, axis=1)
-    keep_k = keep_t[:, :DH].astype(BF16)
     lane3 = lanes((N, 8, LANES))
 
 
@@ -198,10 +204,10 @@
 
     def scores_of(r):
         x = x_ref[r * 256 : (r + 1) * 256, :]
-        return dot(x[:, DH : 2 * DH] * keep_k, x[:, :DH], NT)
+        return dot(x[:, DH : 2 * DH], x[:, :DH], NT)
 
     def attend(r, exp_scores, total):
-        return dot(x_ref[r * 256 : (r + 1) * 256, :][:, 2 * DH : 3 * DH], exp_scores, TN) / total
+        return dot(x_ref[r * 256 : (r + 1) * 256, :], exp_scores, TN)[2 * DH : 3 * DH] / total
 
     coming = scores_of(0)
     prev = None

time: 84 us -> 83.2 us (level)
  no operation moved by 1% of the time
where the time goes in v5:
time: 83.2 us; the launch traced here: 83 us
  blocking collectives  74.3 us (89%)
  Pallas kernels  7.99 us (10%)
    all_to_all x2, blocking collectives, exchange(): return lax.all_to_all(chunks, AXES, split_axis=0, concat_axis=0, tiled=True)  74.3 us
    pallas_call x1, Pallas kernels, pre(): pl.pallas_call(pre_kernel, out_shape=(jax.ShapeDtypeStruct((4096, LANES),...  3.21 us
    pallas_call x1, Pallas kernels, mid(): pl.pallas_call(mid_kernel, out_shape=jax.ShapeDtypeStruct((2048, LANES),...  3.2 us

profile of v5, /device:TPU:1, one launch (start us, length us, event | category | flops | bytes accessed | tf_op | source)
XLA Modules:
  0.0 83.0 jit_solution(136638692202117672)
XLA Ops:
  0.6 3.2 %pre.1 = (bf16[4096,128]{1,0:T(8,128)(2,1)S(1)}, bf16[512,256]{1,0:T(8,128)(2,1)S(1)}, bf16[256,128]{1,0:T(8,128)(2,1)S(1)}, f32[8,256]{1,0:T(8,128)S(1)}) custom-call(bf16[16,16,128]{2,1,0:T(8,128)(2,1)} %pair_ref.1, bf16[128,256]{1,0:T(8,128)(2,1)} %wo_hbm.1, bf16[128,256]{1,0:T(8,128)(2,1)} %wi_hbm.1, s32[256]{0:T(256)} %flags_hbm.1, ...), custom_call_target="tpu_custom_call" | custom-call | tf_op jit(solution)/shard_map/pre/pallas_call | solution.py:127
  3.8 48.1 %all_to_all.22 = bf16[256,16,128]{2,1,0:T(8,128)(2,1)S(1)} all-to-all(bf16[256,16,128]{2,1,0:T(8,128)(2,1)S(1)} %bitcast.10), channel_id=1, replica_groups=mesh['row'=16,'col'=16] {'row','col'}, dimensions={0} | all-to-all | bytes 2097152 | tf_op jit(solution)/shard_map/all_to_all | solution.py:282
  51.9 3.2 %mid.1 = bf16[2048,128]{1,0:T(8,128)(2,1)S(1)} custom-call(f32[8,256]{1,0:T(8,128)S(1)} %get-tuple-element.6.aux_ref, bf16[4096,128]{1,0:T(8,128)(2,1)S(1)} %bitcast.7), custom_call_target="tpu_custom_call" | custom-call | tf_op jit(solution)/shard_map/mid/pallas_call | solution.py:227
  55.1 0.0 copy-start
  55.1 0.0 copy-start.1
  55.2 0.0 copy-start.2
  55.2 0.0 copy-start.3
  55.2 0.0 copy-start.4
  55.2 0.0 copy-start.5
  55.2 26.2 %all_to_all.23 = bf16[256,8,128]{2,1,0:T(8,128)(2,1)S(1)} all-to-all(bf16[256,8,128]{2,1,0:T(8,128)(2,1)S(1)} %bitcast.9), channel_id=1, replica_groups=mesh['row'=16,'col'=16] {'row','col'}, dimensions={0} | all-to-all | bytes 1048576 | tf_op jit(solution)/shard_map/all_to_all | solution.py:282
  81.4 0.0 copy-done
  81.4 0.0 copy-done.1
  81.4 0.0 copy-done.2
  81.4 0.0 copy-done.3
  81.4 0.0 copy-done.4
  81.4 0.0 copy-done.5
  81.4 1.6 %post.1 = (bf16[32,16,256]{2,1,0:T(8,128)(2,1)}, bf16[16,16,128]{2,1,0:T(8,128)(2,1)}) custom-call(bf16[2048,128]{1,0:T(8,128)(2,1)S(1)} %bitcast.8, bf16[32,16,256]{2,1,0:T(8,128)(2,1)S(1)} %copy-done, bf16[16,16,128]{2,1,0:T(8,128)(2,1)S(1)} %copy-done.1, bf16[512,256]{1,0:T(8,128)(2,1)S(1)} %get-tuple-element.8.msa_ref, ...), custom_call_target="tpu_custom_call" | custom-call | tf_op jit(solution)/shard_map/post/pallas_call | solution.py:270
Async XLA Ops:
  55.1 26.2 %copy-start = (bf16[32,16,256]{2,1,0:T(8,128)(2,1)S(1)}, bf16[32,16,256]{2,1,0:T(8,128)(2,1)}, u32[]{:S(2)}) copy-start(bf16[32,16,256]{2,1,0:T(8,128)(2,1)} %homolog_ref.1) | copy-start | bytes 786436
  55.1 26.2 %copy-start.1 = (bf16[16,16,128]{2,1,0:T(8,128)(2,1)S(1)}, bf16[16,16,128]{2,1,0:T(8,128)(2,1)}, u32[]{:S(2)}) copy-start(bf16[16,16,128]{2,1,0:T(8,128)(2,1)} %pair_ref.1) | copy-start | bytes 196612
  55.2 26.2 %copy-start.2 = (bf16[256,256]{1,0:T(8,128)(2,1)S(1)}, bf16[256,256]{1,0:T(8,128)(2,1)}, u32[]{:S(2)}) copy-start(bf16[256,256]{1,0:T(8,128)(2,1)} %wg_ref.1) | copy-start | bytes 393220
  55.2 26.2 %copy-start.3 = (bf16[256,256]{1,0:T(8,128)(2,1)S(1)}, bf16[256,256]{1,0:T(8,128)(2,1)}, u32[]{:S(2)}) copy-start(bf16[256,256]{1,0:T(8,128)(2,1)} %wf_ref.1) | copy-start | bytes 393220
  55.2 26.2 %copy-start.4 = (bf16[128,128]{1,0:T(8,128)(2,1)S(1)}, bf16[128,128]{1,0:T(8,128)(2,1)}, u32[]{:S(2)}) copy-start(bf16[128,128]{1,0:T(8,128)(2,1)} %wtg_ref.1) | copy-start | bytes 98308
  55.2 26.2 %copy-start.5 = (bf16[128,128]{1,0:T(8,128)(2,1)S(1)}, bf16[128,128]{1,0:T(8,128)(2,1)}, u32[]{:S(2)}) copy-start(bf16[128,128]{1,0:T(8,128)(2,1)} %wtf_ref.1) | copy-start | bytes 98308

commit v6 on v5

--- a/solution.py
+++ b/solution.py
@@ -74,18 +74,21 @@
         copy.wait()
     pair_norm = standardize(pair_ref[...].reshape(N * N, LANES)).astype(BF16)
     pn_ref[...] = pair_norm
-    for w_ref, first in ((wo_ref, 0), (wi_ref, 8)):
+    lane8 = lanes((LANES, LANES))
+    sides = []
+    for w_ref in (wo_ref, wi_ref):
         projected = dot(pair_norm, w_ref[...])
-        edge = (jax.nn.sigmoid(projected[:, :LANES]) * projected[:, LANES:]).T
-        for k in range(N):
-            half, k8 = k // 8, k % 8
-            flag = flags_ref[row * N + k].astype(F32)
-            part = turn(edge[:, half * LANES : (half + 1) * LANES], 112 - k8 * 16) * flag
-            tri_ref[pl.ds(half * 2048 + first + k8, LANES, stride=16), :] = part
+        sides.append((jax.nn.sigmoid(projected[:, :LANES]) * projected[:, LANES:]).T)
+    for k in range(N):
+        half, k8 = k // 8, k % 8
+        flag = flags_ref[row * N + k].astype(F32)
+        left, right = (side[:, half * LANES : (half + 1) * LANES] for side in sides)
+        part = jnp.where(lane8 < 112, turn(left, 96 - k8 * 16), turn(right, 112 - k8 * 16)) * flag
+        tri_ref[pl.ds(half * 1024 + k8, LANES, stride=8), :] = part
     bias = dot(wb_ref[...], pair_norm, NT)
-    for i in range(N):
-        half, i8 = i // 8, i % 8
-        bias_ref[pl.ds(i, HEADS, stride=16), :] = turn(bias[:, half * LANES : (half + 1) * LANES], 96 - i8 * 16)
+    for i in range(8):
+        part = jnp.where(lane8[:8] < 112, turn(bias[:, :LANES], 96 - i * 16), turn(bias[:, LANES:], 112 - i * 16))
+        bias_ref[pl.ds(i, HEADS, stride=8), :] = part
 
     lane = lanes((512, LANES))
     tile_row = lax.broadcasted_iota(jnp.int32, (N, LANES), 0)
@@ -104,10 +107,10 @@
         both = dot(msa_norm, jnp.concatenate(parts, axis=1))
         for head in (h, h + 1):
             y = both[:, (head - h) * LANES : (head - h + 1) * LANES]
-            bias_h = bias_ref[head * 16 : (head + 1) * 16, :]
-            bias_h = jnp.broadcast_to(bias_h[None], (32, 16, LANES)).reshape(512, LANES)
-            tri = tri_ref[head * 512 : (head + 1) * 512, :]
-            out = jnp.where(lane < 96, y * factor, jnp.where(lane < 112, bias_h, tri))
+            tri = tri_ref[head * 256 : (head + 1) * 256, :].reshape(32, 8, LANES)
+            bias_h = jnp.broadcast_to(bias_ref[head * 8 : (head + 1) * 8, :][None], (32, 8, LANES))
+            tail = jnp.stack([tri, bias_h], axis=1).reshape(512, LANES)
+            out = jnp.where(lane < 96, y * factor, tail)
             send_ref[head * 512 : (head + 1) * 512, :] = out.astype(BF16)
     aux_ref[0:1, :] = flags2_ref[...].astype(F32)
     aux_ref[1:2, :] = chain_ref[...].astype(F32)
@@ -135,16 +138,23 @@
         in_specs=[HBM] * 11,
         out_specs=(VMEM, VMEM, VMEM, VMEM),
         scratch_shapes=scratch_like(*operands)
-        + [pltpu.VMEM((4096, LANES), F32), pltpu.VMEM((LANES, LANES), F32), pltpu.SemaphoreType.DMA((11,))],
+        + [pltpu.VMEM((2048, LANES), F32), pltpu.VMEM((HEADS * 8, LANES), F32), pltpu.SemaphoreType.DMA((11,))],
         compiler_params=pltpu.CompilerParams(vmem_limit_bytes=32 * 2**20),
         name="pre",
     )(*in_hbm(*operands))
 
 
-def mid_kernel(aux_ref, x_ref, out_ref, ps_ref):
+def mid_kernel(aux_ref, x_ref, out_ref, ps_ref, scores_ref):
     wide = (256, LANES)
     slot = lanes(wide) // 16
-    bias_cols, tri_cols = [], []
+    def key_query(r):
+        x = x_ref[r * 256 : (r + 1) * 256, :]
+        return dot(x[:, DH : 2 * DH], x[:, :DH], NT)
+
+    for r in range(N):
+        scores_ref[r] = key_query(r)
+
+    firsts, seconds = [], []
     for half in range(2):
         kept = [None, None]
         for c8 in range(8):
@@ -155,12 +165,13 @@
             pair_slots = (slot == c8) | (slot == (c8 + 1) % 8)
             kept[c8 % 2] = part if old is None else jnp.where(pair_slots, part, old)
         even = slot % 2 == 0
-        bias_cols.append(jnp.where(even, kept[0], kept[1]))
-        tri_cols.append(turn(jnp.where(even, kept[1], kept[0]), -16))
-    bias = jnp.concatenate(bias_cols, axis=1)
-    tri = jnp.concatenate(tri_cols, axis=1).reshape(N, 2, 8, 256)
-    left = tri[:, 0].reshape(LANES, 256).T.astype(BF16)
-    right = tri[:, 1].reshape(LANES, 256).astype(BF16)
+        firsts.append(jnp.where(even, kept[0], kept[1]))
+        seconds.append(turn(jnp.where(even, kept[1], kept[0]), -16))
+    first = jnp.concatenate(firsts, axis=1).reshape(N, 2, 8, 256)
+    second = jnp.concatenate(seconds, axis=1).reshape(N, 2, 8, 256)
+    bias = jnp.stack([first[:, 1], second[:, 1]], axis=1).reshape(256, 256)
+    left = first[:, 0].reshape(LANES, 256).T.astype(BF16)
+    right = second[:, 0].reshape(LANES, 256).astype(BF16)
     product = dot(left, right)
     high = product.astype(BF16).astype(F32)
     rest = product - high
@@ -202,19 +213,15 @@
         chunk = jnp.where(lane3 % 64 < DH, chunk, ps_ref[:, r])
         out_ref[r * LANES : (r + 1) * LANES, :] = chunk.reshape(LANES, LANES).astype(BF16)
 
-    def scores_of(r):
-        x = x_ref[r * 256 : (r + 1) * 256, :]
-        return dot(x[:, DH : 2 * DH], x[:, :DH], NT)
-
     def attend(r, exp_scores, total):
         return dot(x_ref[r * 256 : (r + 1) * 256, :], exp_scores, TN)[2 * DH : 3 * DH] / total
 
-    coming = scores_of(0)
+    coming = scores_ref[0]
     prev = None
     for r in range(N):
         scores = coming + extra
         if r + 1 < N:
-            coming = scores_of(r + 1)
+            coming = scores_ref[r + 1]
         exp_scores = jnp.exp(scores - jnp.max(scores, axis=0, keepdims=True))
         total = jnp.sum(exp_scores, axis=0, keepdims=True)
         if prev is not None:
@@ -229,7 +236,7 @@
         out_shape=jax.ShapeDtypeStruct((2048, LANES), BF16),
         in_specs=[VMEM] * 2,
         out_specs=VMEM,
-        scratch_shapes=[pltpu.VMEM((N, N, 8, LANES), F32)],
+        scratch_shapes=[pltpu.VMEM((N, N, 8, LANES), F32), pltpu.VMEM((N, 256, 256), F32)],
         compiler_params=pltpu.CompilerParams(vmem_limit_bytes=32 * 2**20),
         name="mid",
     )(aux, received)

time: 83.2 us -> 82.4 us (level)
  no operation moved by 1% of the time
where the time goes in v6:
time: 82.4 us; the launch traced here: 82.2 us
  blocking collectives  74.2 us (90%)
  Pallas kernels  7.21 us (9%)
    all_to_all x2, blocking collectives, exchange(): return lax.all_to_all(chunks, AXES, split_axis=0, concat_axis=0, tiled=True)  74.2 us
    pallas_call x1, Pallas kernels, pre(): pl.pallas_call(pre_kernel, out_shape=(jax.ShapeDtypeStruct((4096, LANES),...  2.91 us
    pallas_call x1, Pallas kernels, mid(): pl.pallas_call(mid_kernel, out_shape=jax.ShapeDtypeStruct((2048, LANES),...  2.73 us

profile of v6, /device:TPU:1, one launch (start us, length us, event | category | flops | bytes accessed | tf_op | source)
XLA Modules:
  0.0 82.2 jit_solution(6147779827220565987)
XLA Ops:
  0.6 2.9 %pre.1 = (bf16[4096,128]{1,0:T(8,128)(2,1)S(1)}, bf16[512,256]{1,0:T(8,128)(2,1)S(1)}, bf16[256,128]{1,0:T(8,128)(2,1)S(1)}, f32[8,256]{1,0:T(8,128)S(1)}) custom-call(bf16[16,16,128]{2,1,0:T(8,128)(2,1)} %pair_ref.1, bf16[128,256]{1,0:T(8,128)(2,1)} %wo_hbm.1, bf16[128,256]{1,0:T(8,128)(2,1)} %wi_hbm.1, s32[256]{0:T(256)} %flags_hbm.1, ...), custom_call_target="tpu_custom_call" | custom-call | tf_op jit(solution)/shard_map/pre/pallas_call | solution.py:130
  3.5 48.1 %all_to_all.22 = bf16[256,16,128]{2,1,0:T(8,128)(2,1)S(1)} all-to-all(bf16[256,16,128]{2,1,0:T(8,128)(2,1)S(1)} %bitcast.10), channel_id=1, replica_groups=mesh['row'=16,'col'=16] {'row','col'}, dimensions={0} | all-to-all | bytes 2097152 | tf_op jit(solution)/shard_map/all_to_all | solution.py:289
  51.6 2.7 %mid.1 = bf16[2048,128]{1,0:T(8,128)(2,1)S(1)} custom-call(f32[8,256]{1,0:T(8,128)S(1)} %get-tuple-element.6.aux_ref, bf16[4096,128]{1,0:T(8,128)(2,1)S(1)} %bitcast.7), custom_call_target="tpu_custom_call" | custom-call | tf_op jit(solution)/shard_map/mid/pallas_call | solution.py:234
  54.3 0.0 copy-start
  54.4 0.0 copy-start.1
  54.4 0.0 copy-start.2
  54.4 0.0 copy-start.3
  54.4 0.0 copy-start.4
  54.4 0.0 copy-start.5
  54.4 26.2 %all_to_all.23 = bf16[256,8,128]{2,1,0:T(8,128)(2,1)S(1)} all-to-all(bf16[256,8,128]{2,1,0:T(8,128)(2,1)S(1)} %bitcast.9), channel_id=1, replica_groups=mesh['row'=16,'col'=16] {'row','col'}, dimensions={0} | all-to-all | bytes 1048576 | tf_op jit(solution)/shard_map/all_to_all | solution.py:289
  80.6 0.0 copy-done
  80.6 0.0 copy-done.1
  80.6 0.0 copy-done.2
  80.6 0.0 copy-done.3
  80.6 0.0 copy-done.4
  80.6 0.0 copy-done.5
  80.6 1.6 %post.1 = (bf16[32,16,256]{2,1,0:T(8,128)(2,1)}, bf16[16,16,128]{2,1,0:T(8,128)(2,1)}) custom-call(bf16[2048,128]{1,0:T(8,128)(2,1)S(1)} %bitcast.8, bf16[32,16,256]{2,1,0:T(8,128)(2,1)S(1)} %copy-done, bf16[16,16,128]{2,1,0:T(8,128)(2,1)S(1)} %copy-done.1, bf16[512,256]{1,0:T(8,128)(2,1)S(1)} %get-tuple-element.8.msa_ref, ...), custom_call_target="tpu_custom_call" | custom-call | tf_op jit(solution)/shard_map/post/pallas_call | solution.py:277
Async XLA Ops:
  54.3 26.3 %copy-start = (bf16[32,16,256]{2,1,0:T(8,128)(2,1)S(1)}, bf16[32,16,256]{2,1,0:T(8,128)(2,1)}, u32[]{:S(2)}) copy-start(bf16[32,16,256]{2,1,0:T(8,128)(2,1)} %homolog_ref.1) | copy-start | bytes 786436
  54.4 26.2 %copy-start.1 = (bf16[16,16,128]{2,1,0:T(8,128)(2,1)S(1)}, bf16[16,16,128]{2,1,0:T(8,128)(2,1)}, u32[]{:S(2)}) copy-start(bf16[16,16,128]{2,1,0:T(8,128)(2,1)} %pair_ref.1) | copy-start | bytes 196612
  54.4 26.2 %copy-start.2 = (bf16[256,256]{1,0:T(8,128)(2,1)S(1)}, bf16[256,256]{1,0:T(8,128)(2,1)}, u32[]{:S(2)}) copy-start(bf16[256,256]{1,0:T(8,128)(2,1)} %wg_ref.1) | copy-start | bytes 393220
  54.4 26.2 %copy-start.3 = (bf16[256,256]{1,0:T(8,128)(2,1)S(1)}, bf16[256,256]{1,0:T(8,128)(2,1)}, u32[]{:S(2)}) copy-start(bf16[256,256]{1,0:T(8,128)(2,1)} %wf_ref.1) | copy-start | bytes 393220
  54.4 26.2 %copy-start.4 = (bf16[128,128]{1,0:T(8,128)(2,1)S(1)}, bf16[128,128]{1,0:T(8,128)(2,1)}, u32[]{:S(2)}) copy-start(bf16[128,128]{1,0:T(8,128)(2,1)} %wtg_ref.1) | copy-start | bytes 98308
  54.4 26.2 %copy-start.5 = (bf16[128,128]{1,0:T(8,128)(2,1)S(1)}, bf16[128,128]{1,0:T(8,128)(2,1)}, u32[]{:S(2)}) copy-start(bf16[128,128]{1,0:T(8,128)(2,1)} %wtf_ref.1) | copy-start | bytes 98308

commit v7 on v6

--- a/solution.py
+++ b/solution.py
@@ -147,6 +147,7 @@
 def mid_kernel(aux_ref, x_ref, out_ref, ps_ref, scores_ref):
     wide = (256, LANES)
     slot = lanes(wide) // 16
+
     def key_query(r):
         x = x_ref[r * 256 : (r + 1) * 256, :]
         return dot(x[:, DH : 2 * DH], x[:, :DH], NT)
@@ -187,11 +188,11 @@
             part_a = jnp.where(ours, *upper[0])
             part_b = turn(jnp.where(ours, *upper[1]), 64)
             near = (slot8 >= parity) & (slot8 < parity + 4)
-            for merged, firsts in (
+            for merged, columns in (
                 (jnp.where(near, part_a, part_b), (parity, parity + 2)),
                 (jnp.where(near, part_b, part_a), (parity + 4, parity + 6)),
             ):
-                for c8 in firsts:
+                for c8 in columns:
                     ps_ref[half * 8 + c8] = turn(merged, 32 - c8 * 16).reshape(N, 8, LANES)
 
     chain = jnp.broadcast_to(aux_ref[1:2, :], (LANES, 256))
@@ -205,7 +206,6 @@
         extra.append(jnp.where(keep_t > 0.0, bias_t[:, cols] + cross, -1000000000.0))
     extra = jnp.concatenate(extra, axis=1)
     lane3 = lanes((N, 8, LANES))
-
 
     def finish(r, attended):
         both = jnp.concatenate([attended, attended, attended, attended], axis=0).T.reshape(N, 2, 8, LANES)
@@ -260,13 +260,12 @@
 
     t = x.reshape(256, 8, LANES)
     t = t[:LANES] + t[LANES:]
-    t = t + turn(t, -16)
     t_ref[...] = t.reshape(1024, LANES)
     upper, lower = [], []
     for i8 in range(8):
         rows = t_ref[pl.ds(i8, LANES, stride=8), :].T
-        upper.append(rows[32:48])
-        lower.append(rows[96:112])
+        upper.append(rows[32:48] + rows[48:64])
+        lower.append(rows[96:112] + rows[112:128])
     product_norm = standardize(jnp.concatenate(upper + lower, axis=0)).astype(BF16)
     update = jax.nn.sigmoid(dot(pn_ref[...], wtg_ref[...])) * dot(product_norm, wtf_ref[...])
     pair_out = pair_ref[...].reshape(N * N, LANES).astype(F32) + update

time: 82.4 us -> 82.4 us (level)
  no operation moved by 1% of the time
where the time goes in v7:
time: 82.4 us; the launch traced here: 82.2 us
  blocking collectives  74.2 us (90%)
  Pallas kernels  7.2 us (9%)
    all_to_all x2, blocking collectives, exchange(): return lax.all_to_all(chunks, AXES, split_axis=0, concat_axis=0, tiled=True)  74.2 us
    pallas_call x1, Pallas kernels, pre(): pl.pallas_call(pre_kernel, out_shape=(jax.ShapeDtypeStruct((4096, LANES),...  2.91 us
    pallas_call x1, Pallas kernels, mid(): pl.pallas_call(mid_kernel, out_shape=jax.ShapeDtypeStruct((2048, LANES),...  2.73 us

profile of v7, /device:TPU:1, one launch (start us, length us, event | category | flops | bytes accessed | tf_op | source)
XLA Modules:
  0.0 82.2 jit_solution(12040034585695560966)
XLA Ops:
  0.6 2.9 %pre.1 = (bf16[4096,128]{1,0:T(8,128)(2,1)S(1)}, bf16[512,256]{1,0:T(8,128)(2,1)S(1)}, bf16[256,128]{1,0:T(8,128)(2,1)S(1)}, f32[8,256]{1,0:T(8,128)S(1)}) custom-call(bf16[16,16,128]{2,1,0:T(8,128)(2,1)} %pair_ref.1, bf16[128,256]{1,0:T(8,128)(2,1)} %wo_hbm.1, bf16[128,256]{1,0:T(8,128)(2,1)} %wi_hbm.1, s32[256]{0:T(256)} %flags_hbm.1, ...), custom_call_target="tpu_custom_call" | custom-call | tf_op jit(solution)/shard_map/pre/pallas_call | solution.py:130
  3.5 48.1 %all_to_all.22 = bf16[256,16,128]{2,1,0:T(8,128)(2,1)S(1)} all-to-all(bf16[256,16,128]{2,1,0:T(8,128)(2,1)S(1)} %bitcast.10), channel_id=1, replica_groups=mesh['row'=16,'col'=16] {'row','col'}, dimensions={0} | all-to-all | bytes 2097152 | tf_op jit(solution)/shard_map/all_to_all | solution.py:288
  51.6 2.7 %mid.1 = bf16[2048,128]{1,0:T(8,128)(2,1)S(1)} custom-call(f32[8,256]{1,0:T(8,128)S(1)} %get-tuple-element.6.aux_ref, bf16[4096,128]{1,0:T(8,128)(2,1)S(1)} %bitcast.7), custom_call_target="tpu_custom_call" | custom-call | tf_op jit(solution)/shard_map/mid/pallas_call | solution.py:234
  54.3 0.0 copy-start
  54.4 0.0 copy-start.1
  54.4 0.0 copy-start.2
  54.4 0.0 copy-start.3
  54.4 0.0 copy-start.4
  54.4 0.0 copy-start.5
  54.4 26.2 %all_to_all.23 = bf16[256,8,128]{2,1,0:T(8,128)(2,1)S(1)} all-to-all(bf16[256,8,128]{2,1,0:T(8,128)(2,1)S(1)} %bitcast.9), channel_id=1, replica_groups=mesh['row'=16,'col'=16] {'row','col'}, dimensions={0} | all-to-all | bytes 1048576 | tf_op jit(solution)/shard_map/all_to_all | solution.py:288
  80.6 0.0 copy-done
  80.6 0.0 copy-done.1
  80.6 0.0 copy-done.2
  80.6 0.0 copy-done.3
  80.6 0.0 copy-done.4
  80.6 0.0 copy-done.5
  80.6 1.6 %post.1 = (bf16[32,16,256]{2,1,0:T(8,128)(2,1)}, bf16[16,16,128]{2,1,0:T(8,128)(2,1)}) custom-call(bf16[2048,128]{1,0:T(8,128)(2,1)S(1)} %bitcast.8, bf16[32,16,256]{2,1,0:T(8,128)(2,1)S(1)} %copy-done, bf16[16,16,128]{2,1,0:T(8,128)(2,1)S(1)} %copy-done.1, bf16[512,256]{1,0:T(8,128)(2,1)S(1)} %get-tuple-element.8.msa_ref, ...), custom_call_target="tpu_custom_call" | custom-call | tf_op jit(solution)/shard_map/post/pallas_call | solution.py:276
Async XLA Ops:
  54.3 26.3 %copy-start = (bf16[32,16,256]{2,1,0:T(8,128)(2,1)S(1)}, bf16[32,16,256]{2,1,0:T(8,128)(2,1)}, u32[]{:S(2)}) copy-start(bf16[32,16,256]{2,1,0:T(8,128)(2,1)} %homolog_ref.1) | copy-start | bytes 786436
  54.4 26.2 %copy-start.1 = (bf16[16,16,128]{2,1,0:T(8,128)(2,1)S(1)}, bf16[16,16,128]{2,1,0:T(8,128)(2,1)}, u32[]{:S(2)}) copy-start(bf16[16,16,128]{2,1,0:T(8,128)(2,1)} %pair_ref.1) | copy-start | bytes 196612
  54.4 26.2 %copy-start.2 = (bf16[256,256]{1,0:T(8,128)(2,1)S(1)}, bf16[256,256]{1,0:T(8,128)(2,1)}, u32[]{:S(2)}) copy-start(bf16[256,256]{1,0:T(8,128)(2,1)} %wg_ref.1) | copy-start | bytes 393220
  54.4 26.2 %copy-start.3 = (bf16[256,256]{1,0:T(8,128)(2,1)S(1)}, bf16[256,256]{1,0:T(8,128)(2,1)}, u32[]{:S(2)}) copy-start(bf16[256,256]{1,0:T(8,128)(2,1)} %wf_ref.1) | copy-start | bytes 393220
  54.4 26.2 %copy-start.4 = (bf16[128,128]{1,0:T(8,128)(2,1)S(1)}, bf16[128,128]{1,0:T(8,128)(2,1)}, u32[]{:S(2)}) copy-start(bf16[128,128]{1,0:T(8,128)(2,1)} %wtg_ref.1) | copy-start | bytes 98308
  54.4 26.2 %copy-start.5 = (bf16[128,128]{1,0:T(8,128)(2,1)S(1)}, bf16[128,128]{1,0:T(8,128)(2,1)}, u32[]{:S(2)}) copy-start(bf16[128,128]{1,0:T(8,128)(2,1)} %wtf_ref.1) | copy-start | bytes 98308

commit v8 on v7

--- a/solution.py
+++ b/solution.py
@@ -218,6 +218,7 @@
 
     coming = scores_ref[0]
     prev = None
+    done = []
     for r in range(N):
         scores = coming + extra
         if r + 1 < N:
@@ -225,9 +226,11 @@
         exp_scores = jnp.exp(scores - jnp.max(scores, axis=0, keepdims=True))
         total = jnp.sum(exp_scores, axis=0, keepdims=True)
         if prev is not None:
-            finish(r - 1, attend(r - 1, *prev))
+            done.append(attend(r - 1, *prev))
         prev = (exp_scores.astype(BF16), total)
-    finish(N - 1, attend(N - 1, *prev))
+    done.append(attend(N - 1, *prev))
+    for r in range(N):
+        finish(r, done[r])
 
 
 def mid(received, aux):

time: 82.4 us -> 82.2 us (level)
  no operation moved by 1% of the time
where the time goes in v8:
time: 82.2 us; the launch traced here: 82 us
  blocking collectives  74.2 us (90%)
  Pallas kernels  7.01 us (9%)
    all_to_all x2, blocking collectives, exchange(): return lax.all_to_all(chunks, AXES, split_axis=0, concat_axis=0, tiled=True)  74.2 us
    pallas_call x1, Pallas kernels, pre(): pl.pallas_call(pre_kernel, out_shape=(jax.ShapeDtypeStruct((4096, LANES),...  2.91 us
    pallas_call x1, Pallas kernels, mid(): pl.pallas_call(mid_kernel, out_shape=jax.ShapeDtypeStruct((2048, LANES),...  2.54 us

profile of v8, /device:TPU:1, one launch (start us, length us, event | category | flops | bytes accessed | tf_op | source)
XLA Modules:
  0.0 82.0 jit_solution(9295761944848744713)
XLA Ops:
  0.6 2.9 %pre.1 = (bf16[4096,128]{1,0:T(8,128)(2,1)S(1)}, bf16[512,256]{1,0:T(8,128)(2,1)S(1)}, bf16[256,128]{1,0:T(8,128)(2,1)S(1)}, f32[8,256]{1,0:T(8,128)S(1)}) custom-call(bf16[16,16,128]{2,1,0:T(8,128)(2,1)} %pair_ref.1, bf16[128,256]{1,0:T(8,128)(2,1)} %wo_hbm.1, bf16[128,256]{1,0:T(8,128)(2,1)} %wi_hbm.1, s32[256]{0:T(256)} %flags_hbm.1, ...), custom_call_target="tpu_custom_call" | custom-call | tf_op jit(solution)/shard_map/pre/pallas_call | solution.py:130
  3.5 48.1 %all_to_all.22 = bf16[256,16,128]{2,1,0:T(8,128)(2,1)S(1)} all-to-all(bf16[256,16,128]{2,1,0:T(8,128)(2,1)S(1)} %bitcast.10), channel_id=1, replica_groups=mesh['row'=16,'col'=16] {'row','col'}, dimensions={0} | all-to-all | bytes 2097152 | tf_op jit(solution)/shard_map/all_to_all | solution.py:291
  51.6 2.5 %mid.1 = bf16[2048,128]{1,0:T(8,128)(2,1)S(1)} custom-call(f32[8,256]{1,0:T(8,128)S(1)} %get-tuple-element.6.aux_ref, bf16[4096,128]{1,0:T(8,128)(2,1)S(1)} %bitcast.7), custom_call_target="tpu_custom_call" | custom-call | tf_op jit(solution)/shard_map/mid/pallas_call | solution.py:237
  54.2 0.0 copy-start
  54.2 0.0 copy-start.1
  54.2 0.0 copy-start.2
  54.2 0.0 copy-start.3
  54.2 0.0 copy-start.4
  54.2 0.0 copy-start.5
  54.2 26.2 %all_to_all.23 = bf16[256,8,128]{2,1,0:T(8,128)(2,1)S(1)} all-to-all(bf16[256,8,128]{2,1,0:T(8,128)(2,1)S(1)} %bitcast.9), channel_id=1, replica_groups=mesh['row'=16,'col'=16] {'row','col'}, dimensions={0} | all-to-all | bytes 1048576 | tf_op jit(solution)/shard_map/all_to_all | solution.py:291
  80.4 0.0 copy-done
  80.4 0.0 copy-done.1
  80.4 0.0 copy-done.2
  80.4 0.0 copy-done.3
  80.4 0.0 copy-done.4
  80.4 0.0 copy-done.5
  80.4 1.6 %post.1 = (bf16[32,16,256]{2,1,0:T(8,128)(2,1)}, bf16[16,16,128]{2,1,0:T(8,128)(2,1)}) custom-call(bf16[2048,128]{1,0:T(8,128)(2,1)S(1)} %bitcast.8, bf16[32,16,256]{2,1,0:T(8,128)(2,1)S(1)} %copy-done, bf16[16,16,128]{2,1,0:T(8,128)(2,1)S(1)} %copy-done.1, bf16[512,256]{1,0:T(8,128)(2,1)S(1)} %get-tuple-element.8.msa_ref, ...), custom_call_target="tpu_custom_call" | custom-call | tf_op jit(solution)/shard_map/post/pallas_call | solution.py:279
Async XLA Ops:
  54.2 26.3 %copy-start = (bf16[32,16,256]{2,1,0:T(8,128)(2,1)S(1)}, bf16[32,16,256]{2,1,0:T(8,128)(2,1)}, u32[]{:S(2)}) copy-start(bf16[32,16,256]{2,1,0:T(8,128)(2,1)} %homolog_ref.1) | copy-start | bytes 786436
  54.2 26.2 %copy-start.1 = (bf16[16,16,128]{2,1,0:T(8,128)(2,1)S(1)}, bf16[16,16,128]{2,1,0:T(8,128)(2,1)}, u32[]{:S(2)}) copy-start(bf16[16,16,128]{2,1,0:T(8,128)(2,1)} %pair_ref.1) | copy-start | bytes 196612
  54.2 26.2 %copy-start.2 = (bf16[256,256]{1,0:T(8,128)(2,1)S(1)}, bf16[256,256]{1,0:T(8,128)(2,1)}, u32[]{:S(2)}) copy-start(bf16[256,256]{1,0:T(8,128)(2,1)} %wg_ref.1) | copy-start | bytes 393220
  54.2 26.2 %copy-start.3 = (bf16[256,256]{1,0:T(8,128)(2,1)S(1)}, bf16[256,256]{1,0:T(8,128)(2,1)}, u32[]{:S(2)}) copy-start(bf16[256,256]{1,0:T(8,128)(2,1)} %wf_ref.1) | copy-start | bytes 393220
  54.2 26.2 %copy-start.4 = (bf16[128,128]{1,0:T(8,128)(2,1)S(1)}, bf16[128,128]{1,0:T(8,128)(2,1)}, u32[]{:S(2)}) copy-start(bf16[128,128]{1,0:T(8,128)(2,1)} %wtg_ref.1) | copy-start | bytes 98308
  54.2 26.2 %copy-start.5 = (bf16[128,128]{1,0:T(8,128)(2,1)S(1)}, bf16[128,128]{1,0:T(8,128)(2,1)}, u32[]{:S(2)}) copy-start(bf16[128,128]{1,0:T(8,128)(2,1)} %wtf_ref.1) | copy-start | bytes 98308

commit v9 on v8

--- a/solution.py
+++ b/solution.py
@@ -208,7 +208,8 @@
     lane3 = lanes((N, 8, LANES))
 
     def finish(r, attended):
-        both = jnp.concatenate([attended, attended, attended, attended], axis=0).T.reshape(N, 2, 8, LANES)
+        attended = attended.astype(BF16)
+        both = jnp.concatenate([attended, attended, attended, attended], axis=0).T.astype(F32).reshape(N, 2, 8, LANES)
         chunk = jnp.where(lane3 < 64, both[:, 0], both[:, 1])
         chunk = jnp.where(lane3 % 64 < DH, chunk, ps_ref[:, r])
         out_ref[r * LANES : (r + 1) * LANES, :] = chunk.reshape(LANES, LANES).astype(BF16)

time: 82.2 us -> 82.1 us (level)
  no operation moved by 1% of the time
where the time goes in v9:
time: 82.1 us; the launch traced here: 82 us
  blocking collectives  74.2 us (90%)
  Pallas kernels  6.97 us (8%)
    all_to_all x2, blocking collectives, exchange(): return lax.all_to_all(chunks, AXES, split_axis=0, concat_axis=0, tiled=True)  74.2 us
    pallas_call x1, Pallas kernels, pre(): pl.pallas_call(pre_kernel, out_shape=(jax.ShapeDtypeStruct((4096, LANES),...  2.91 us
    pallas_call x1, Pallas kernels, mid(): pl.pallas_call(mid_kernel, out_shape=jax.ShapeDtypeStruct((2048, LANES),...  2.5 us

profile of v9, /device:TPU:1, one launch (start us, length us, event | category | flops | bytes accessed | tf_op | source)
XLA Modules:
  0.0 82.0 jit_solution(6719916243656193998)
XLA Ops:
  0.6 2.9 %pre.1 = (bf16[4096,128]{1,0:T(8,128)(2,1)S(1)}, bf16[512,256]{1,0:T(8,128)(2,1)S(1)}, bf16[256,128]{1,0:T(8,128)(2,1)S(1)}, f32[8,256]{1,0:T(8,128)S(1)}) custom-call(bf16[16,16,128]{2,1,0:T(8,128)(2,1)} %pair_ref.1, bf16[128,256]{1,0:T(8,128)(2,1)} %wo_hbm.1, bf16[128,256]{1,0:T(8,128)(2,1)} %wi_hbm.1, s32[256]{0:T(256)} %flags_hbm.1, ...), custom_call_target="tpu_custom_call" | custom-call | tf_op jit(solution)/shard_map/pre/pallas_call | solution.py:130
  3.5 48.1 %all_to_all.22 = bf16[256,16,128]{2,1,0:T(8,128)(2,1)S(1)} all-to-all(bf16[256,16,128]{2,1,0:T(8,128)(2,1)S(1)} %bitcast.10), channel_id=1, replica_groups=mesh['row'=16,'col'=16] {'row','col'}, dimensions={0} | all-to-all | bytes 2097152 | tf_op jit(solution)/shard_map/all_to_all | solution.py:292
  51.6 2.5 %mid.1 = bf16[2048,128]{1,0:T(8,128)(2,1)S(1)} custom-call(f32[8,256]{1,0:T(8,128)S(1)} %get-tuple-element.6.aux_ref, bf16[4096,128]{1,0:T(8,128)(2,1)S(1)} %bitcast.7), custom_call_target="tpu_custom_call" | custom-call | tf_op jit(solution)/shard_map/mid/pallas_call | solution.py:238
  54.1 0.0 copy-start
  54.1 0.0 copy-start.1
  54.1 0.0 copy-start.2
  54.2 0.0 copy-start.3
  54.2 0.0 copy-start.4
  54.2 0.0 copy-start.5
  54.2 26.2 %all_to_all.23 = bf16[256,8,128]{2,1,0:T(8,128)(2,1)S(1)} all-to-all(bf16[256,8,128]{2,1,0:T(8,128)(2,1)S(1)} %bitcast.9), channel_id=1, replica_groups=mesh['row'=16,'col'=16] {'row','col'}, dimensions={0} | all-to-all | bytes 1048576 | tf_op jit(solution)/shard_map/all_to_all | solution.py:292
  80.4 0.0 copy-done
  80.4 0.0 copy-done.1
  80.4 0.0 copy-done.2
  80.4 0.0 copy-done.3
  80.4 0.0 copy-done.4
  80.4 0.0 copy-done.5
  80.4 1.6 %post.1 = (bf16[32,16,256]{2,1,0:T(8,128)(2,1)}, bf16[16,16,128]{2,1,0:T(8,128)(2,1)}) custom-call(bf16[2048,128]{1,0:T(8,128)(2,1)S(1)} %bitcast.8, bf16[32,16,256]{2,1,0:T(8,128)(2,1)S(1)} %copy-done, bf16[16,16,128]{2,1,0:T(8,128)(2,1)S(1)} %copy-done.1, bf16[512,256]{1,0:T(8,128)(2,1)S(1)} %get-tuple-element.8.msa_ref, ...), custom_call_target="tpu_custom_call" | custom-call | tf_op jit(solution)/shard_map/post/pallas_call | solution.py:280
Async XLA Ops:
  54.1 26.3 %copy-start = (bf16[32,16,256]{2,1,0:T(8,128)(2,1)S(1)}, bf16[32,16,256]{2,1,0:T(8,128)(2,1)}, u32[]{:S(2)}) copy-start(bf16[32,16,256]{2,1,0:T(8,128)(2,1)} %homolog_ref.1) | copy-start | bytes 786436
  54.1 26.2 %copy-start.1 = (bf16[16,16,128]{2,1,0:T(8,128)(2,1)S(1)}, bf16[16,16,128]{2,1,0:T(8,128)(2,1)}, u32[]{:S(2)}) copy-start(bf16[16,16,128]{2,1,0:T(8,128)(2,1)} %pair_ref.1) | copy-start | bytes 196612
  54.1 26.2 %copy-start.2 = (bf16[256,256]{1,0:T(8,128)(2,1)S(1)}, bf16[256,256]{1,0:T(8,128)(2,1)}, u32[]{:S(2)}) copy-start(bf16[256,256]{1,0:T(8,128)(2,1)} %wg_ref.1) | copy-start | bytes 393220
  54.2 26.2 %copy-start.3 = (bf16[256,256]{1,0:T(8,128)(2,1)S(1)}, bf16[256,256]{1,0:T(8,128)(2,1)}, u32[]{:S(2)}) copy-start(bf16[256,256]{1,0:T(8,128)(2,1)} %wf_ref.1) | copy-start | bytes 393220
  54.2 26.2 %copy-start.4 = (bf16[128,128]{1,0:T(8,128)(2,1)S(1)}, bf16[128,128]{1,0:T(8,128)(2,1)}, u32[]{:S(2)}) copy-start(bf16[128,128]{1,0:T(8,128)(2,1)} %wtg_ref.1) | copy-start | bytes 98308
  54.2 26.2 %copy-start.5 = (bf16[128,128]{1,0:T(8,128)(2,1)S(1)}, bf16[128,128]{1,0:T(8,128)(2,1)}, u32[]{:S(2)}) copy-start(bf16[128,128]{1,0:T(8,128)(2,1)} %wtf_ref.1) | copy-start | bytes 98308
